TPU v7x, 32 devices: a whole 2x2x4 slice. The times are simulated.
32 devices in a mesh: row: 8 (over z, core), col: 4 (over y, x).
Axes of the slice: x: 2, y: 2, z: 4, core: 2. Of those that a mesh axis runs over, the one named last changes fastest.
Arguments:
- tokens: bfloat16 [1024, 12288], P('row', 'col'), may hold values from -6 to 6
- weight: bfloat16 [12288, 24576], P('col', 'row'), may hold values from -0.0546875 to 0.0546875
- cotangent: bfloat16 [1024, 24576], P('col', 'row'), may hold values from -6 to 6
Outputs:
- hidden: bfloat16 [1024, 24576], P('col', 'row')
- grad_weight: float32 [12288, 24576], P('col', 'row')
- grad_tokens: bfloat16 [1024, 12288], P('row', 'col')
All inputs are finite; a program needn't handle non-finite values.
Results may differ from a plain program's by a relative error of at most 0.0049.
Values may be sent and summed in bfloat16 or wider, within the bound.
A program may use at most 192 MiB of HBM per device.

v0:
```python
import math

import jax
import jax.numpy as jnp
from jax import lax
from jax.sharding import PartitionSpec as P


def gelu_exact(value):
    return 0.5 * value * (1.0 + jax.scipy.special.erf(value / math.sqrt(2.0)))


def gelu_slope(value):
    cumulative = 0.5 * (1.0 + jax.scipy.special.erf(value / math.sqrt(2.0)))
    return cumulative + value * jnp.exp(-0.5 * value * value) / math.sqrt(2.0 * math.pi)


def shards(tokens, weight, cotangent):
    gathered = lax.all_gather(tokens, "row", axis=0, tiled=True)
    rows = gathered
    pre = lax.psum_scatter(
        jnp.dot(rows, weight, preferred_element_type=jnp.float32),
        "col",
        scatter_dimension=0,
        tiled=True,
    )
    hidden = gelu_exact(pre).astype(jnp.bfloat16)
    grad_pre = (cotangent.astype(jnp.float32) * gelu_slope(pre)).astype(jnp.bfloat16)
    grad_all = lax.all_gather(grad_pre, "col", axis=0, tiled=True)
    grad_weight = lax.dot_general(
        gathered, grad_all, (((0,), (0,)), ((), ())), preferred_element_type=jnp.float32
    )
    rows = grad_all
    grad_tokens = lax.psum_scatter(
        lax.dot_general(rows, weight, (((1,), (1,)), ((), ())), preferred_element_type=jnp.float32),
        "row",
        scatter_dimension=0,
        tiled=True,
    )
    return (hidden, grad_weight, grad_tokens.astype(jnp.bfloat16))


def solution(mesh):
    in_specs = (P("row", "col"), P("col", "row"), P("col", "row"))
    out_specs = (P("col", "row"), P("col", "row"), P("row", "col"))
    return jax.shard_map(shards, mesh=mesh, in_specs=in_specs, out_specs=out_specs, check_vma=False)
```

profile of v0, /device:TPU:0, one launch (start us, length us, event | category | flops | bytes accessed | tf_op | source)
XLA Modules:
  0.0 461.8 jit_solution(18092484596657801216)
XLA Ops:
  7.2 0.0 all-gather.3.cloned.1.call-start
  7.2 0.7 all-gather.3.cloned.1.call-update
  7.9 0.0 reduce-scatter.3.cloned.1.call-start
  7.9 69.2 %all-gather.3.cloned.1.call-done = bf16[1024,3072]{1,0:T(8,128)(2,1)} async-done(((bf16[128,3072]{1,0:T(8,128)(2,1)}), bf16[1024,3072]{1,0:T(8,128)(2,1)}) %all-gather.3.cloned.1.call-update) | async-done | bytes 6291472 | tf_op jit(solution)/shard_map/all_gather | solution.py:19
  77.1 26.1 %fusion.6 = f32[1024,3072]{1,0:T(8,128)} fusion(bf16[1024,3072]{1,0:T(8,128)(2,1)} %all-gather.3.cloned.1.call-done, bf16[3072,3072]{1,0:T(8,128)(2,1)} %param.4), kind=kOutput, calls=%fused_computation.10 | convolution fusion | flops 19327352832 | bytes 37748736 | tf_op jit(solution)/shard_map/dot_general | solution.py:22
  103.2 0.0 copy-start
  103.2 0.0 reduce-scatter.3.cloned.1.call-update
  103.2 0.0 all-gather.5.cloned.1.call-start
  103.3 119.5 %reduce-scatter.3.cloned.1.call-done = f32[256,3072]{1,0:T(8,128)} async-done(((f32[1024,3072]{1,0:T(8,128)}), f32[256,3072]{1,0:T(8,128)}) %reduce-scatter.3.cloned.1.call-update) | async-done | bytes 3145744 | tf_op jit(solution)/shard_map/reduce_scatter | solution.py:21
  222.8 0.0 copy-done
  222.8 4.2 fusion.5
  226.9 0.0 all-gather.5.cloned.1.call-update
  227.0 0.2 reduce-scatter.5.cloned.1.call-start
  227.2 70.1 %all-gather.5.cloned.1.call-done = bf16[1024,3072]{1,0:T(8,128)(2,1)} async-done(((bf16[256,3072]{1,0:T(8,128)(2,1)}), bf16[1024,3072]{1,0:T(8,128)(2,1)}) %all-gather.5.cloned.1.call-update) | async-done | bytes 6291472 | tf_op jit(solution)/shard_map/all_gather | solution.py:29
  297.3 26.2 %fusion.7 = f32[1024,3072]{1,0:T(8,128)} fusion(bf16[1024,3072]{1,0:T(8,128)(2,1)} %all-gather.5.cloned.1.call-done, bf16[3072,3072]{1,0:T(8,128)(2,1)} %param.4), kind=kOutput, calls=%fused_computation.11 | convolution fusion | flops 19327352832 | bytes 37748736 | tf_op jit(solution)/shard_map/dot_general | solution.py:35
  323.5 0.0 reduce-scatter.5.cloned.1.call-update
  323.5 27.7 %convolution_bitcast_fusion = f32[3072,3072]{0,1:T(8,128)} fusion(bf16[1024,3072]{1,0:T(8,128)(2,1)} %all-gather.5.cloned.1.call-done, bf16[1024,3072]{1,0:T(8,128)(2,1)} %all-gather.3.cloned.1.call-done), kind=kOutput, calls=%fused_computation | convolution fusion | flops 19327352832 | bytes 50331648 | tf_op jit(solution)/shard_map/dot_general | solution.py:30
  351.2 37.0 %copy.6 = f32[3072,3072]{1,0:T(8,128)} copy(f32[3072,3072]{0,1:T(8,128)} %convolution_bitcast_fusion) | data formatting | bytes 75497472
  388.2 64.7 %reduce-scatter.5.cloned.1.call-done = f32[128,3072]{1,0:T(8,128)} async-done(((f32[1024,3072]{1,0:T(8,128)}), f32[128,3072]{1,0:T(8,128)}) %reduce-scatter.5.cloned.1.call-update) | async-done | bytes 1572880 | tf_op jit(solution)/shard_map/reduce_scatter | solution.py:34
  452.9 2.4 convert_element_type.15
Async XLA Ops:
  7.2 70.0 %all-gather.3.cloned.1.call-start = ((), (), s32[]{:S(2)}) async-start(), calls=%async_computation.2 | async-start | bytes 7077888 | tf_op jit(solution)/shard_map/all_gather | solution.py:19
  7.9 214.9 %reduce-scatter.3.cloned.1.call-start = ((), (), s32[]{:S(2)}) async-start(), calls=%async_computation.3 | async-start | bytes 15728640 | tf_op jit(solution)/shard_map/reduce_scatter | solution.py:21
  103.2 119.6 %copy-start = (bf16[256,3072]{1,0:T(8,128)(2,1)S(1)}, bf16[256,3072]{1,0:T(8,128)(2,1)}, u32[]{:S(2)}) copy-start(bf16[256,3072]{1,0:T(8,128)(2,1)} %param.5) | copy-start | bytes 4718596
  103.2 194.0 %all-gather.5.cloned.1.call-start = ((), (), s32[]{:S(2)}) async-start(), calls=%async_computation.4 | async-start | bytes 7864320 | tf_op jit(solution)/shard_map/all_gather | solution.py:29
  227.0 225.9 %reduce-scatter.5.cloned.1.call-start = ((), (), s32[]{:S(2)}) async-start(), calls=%async_computation.5 | async-start | bytes 14155776 | tf_op jit(solution)/shard_map/reduce_scatter | solution.py:34
Sparse Core Ops, SparseCore 0:
  9.6 67.4 all-gather.2
  103.3 119.3 reduce-scatter.2
  227.1 70.1 all-gather.4
  323.6 129.1 reduce-scatter.4
where the time goes:
time: 462 us
  waiting for transfers between devices  324 us (70%)
  matrix products  80 us (17%)
  local copies, waits for them, and re-layouts  37 us (8%)
  between operations  13.8 us (3%)
  other arithmetic  6.57 us (1%)
    reduce_scatter x1, waiting for transfers between devices, shards(): lax.psum_scatter(jnp.dot(rows, weight, preferred_element_type=jnp.float32...  119 us
    all_gather x1, waiting for transfers between devices, shards(): grad_all = lax.all_gather(grad_pre, 'col', axis=0, tiled=True)  70.1 us
    all_gather x1, waiting for transfers between devices, shards(): gathered = lax.all_gather(tokens, 'row', axis=0, tiled=True)  69.2 us
    reduce_scatter x1, waiting for transfers between devices, shards(): lax.psum_scatter(lax.dot_general(rows, weight, (((1,), (1,)), ((), ())),...  64.7 us
    unnamed x3, local copies, waits for them, and re-layouts  37 us
    dot_general x1, matrix products, shards(): lax.dot_general(gathered, grad_all, (((0,), (0,)), ((), ())), preferred_e...  27.7 us
    dot_general x1, matrix products, shards(): lax.dot_general(rows, weight, (((1,), (1,)), ((), ())), preferred_element...  26.2 us
    dot_general x1, matrix products, shards(): jnp.dot(rows, weight, preferred_element_type=jnp.float32)  26.1 us
  transfers between devices with their start and end apart: 4, of which 4 were waited for; matrix products, arithmetic and copies ran while one was open for 14% of the time, Pallas kernels for 0%

commit v1 on v0

v1 whole, which is shorter than its diff:
```python
import math

import jax
import jax.numpy as jnp
from jax import lax
from jax.experimental import pallas as pl
from jax.experimental.pallas import tpu as pltpu
from jax.sharding import PartitionSpec as P

PARTS = 2


def gelu_exact(value):
    return 0.5 * value * (1.0 + jax.scipy.special.erf(value / math.sqrt(2.0)))


def gelu_slope(value):
    cumulative = 0.5 * (1.0 + jax.scipy.special.erf(value / math.sqrt(2.0)))
    return cumulative + value * jnp.exp(-0.5 * value * value) / math.sqrt(2.0 * math.pi)


def dot_t_kernel(a_ref, b_ref, out_ref):
    out_ref[...] = lax.dot_general(
        a_ref[...], b_ref[...], (((0,), (0,)), ((), ())), preferred_element_type=jnp.float32
    )


def dot_t(a, b):
    rows, m = a.shape
    n = b.shape[1]
    block = 256
    return pl.pallas_call(
        dot_t_kernel,
        grid=(m // block,),
        in_specs=[
            pl.BlockSpec((rows, block), lambda i: (0, i)),
            pl.BlockSpec((rows, n), lambda i: (0, 0)),
        ],
        out_specs=pl.BlockSpec((block, n), lambda i: (i, 0)),
        out_shape=jax.ShapeDtypeStruct((m, n), jnp.float32),
        compiler_params=pltpu.CompilerParams(vmem_limit_bytes=48 * 1024 * 1024),
        cost_estimate=pl.CostEstimate(
            flops=2 * rows * m * n,
            bytes_accessed=2 * rows * (m + n) + 4 * m * n,
            transcendentals=0,
        ),
    )(a, b)


def swap(value, bit):
    return lax.ppermute(value, "col", [(c, c ^ bit) for c in range(4)])


def pick(value, axis, index):
    return lax.dynamic_index_in_dim(value, index, axis, keepdims=False)


def ordered(mine, other, index, axis):
    first = jnp.where(index == 0, mine, other)
    second = jnp.where(index == 0, other, mine)
    return jnp.stack([first, second], axis)


def scatter_square(partial, x_first):
    me = lax.axis_index("col")
    x, y = me % 2, me // 2
    a = partial.reshape((2, 2) + partial.shape[1:])
    if x_first:
        got = swap(pick(a, 1, 1 - x).astype(jnp.bfloat16), 1)
        a = pick(a, 1, x) + got.astype(jnp.float32)
        got = swap(pick(a, 0, 1 - y).astype(jnp.bfloat16), 2)
        return pick(a, 0, y) + got.astype(jnp.float32)
    got = swap(pick(a, 0, 1 - y).astype(jnp.bfloat16), 2)
    a = pick(a, 0, y) + got.astype(jnp.float32)
    got = swap(pick(a, 0, 1 - x).astype(jnp.bfloat16), 1)
    return pick(a, 0, x) + got.astype(jnp.float32)


def gather_square(value, x_first):
    me = lax.axis_index("col")
    x, y = me % 2, me // 2
    if x_first:
        pair = ordered(value, swap(value, 1), x, 0)
        both = ordered(pair, swap(pair, 2), y, 0)
    else:
        pair = ordered(value, swap(value, 2), y, 0)
        both = ordered(pair, swap(pair, 1), x, 1)
    return both.reshape((4,) + value.shape)


def make(row_n, col_n):
    def shards(tokens, weight, cotangent):
        local, features = tokens.shape
        hidden_n = weight.shape[1]
        owned = cotangent.shape[0]
        sub = local // PARTS
        blocks = owned // local
        square = col_n == 4
        cuts = 2 if square else 1
        wide = hidden_n // cuts
        split = cotangent.reshape(blocks, PARTS, sub, hidden_n)

        gathered = [
            lax.all_gather(tokens[p * sub : (p + 1) * sub], "row", axis=0, tiled=True)
            for p in range(PARTS)
        ]
        hiddens, grads = [], []
        for p in range(PARTS):
            hs, gs = [], []
            for h in range(cuts):
                cols = slice(h * wide, (h + 1) * wide)
                partial = jnp.dot(
                    gathered[p], weight[:, cols], preferred_element_type=jnp.float32
                )
                if square:
                    pre = scatter_square(partial.reshape(col_n, blocks * sub, wide), h == 0)
                else:
                    pre = lax.psum_scatter(partial, "col", scatter_dimension=0, tiled=True)
                cot = split[:, p, :, cols].reshape(blocks * sub, wide)
                hs.append(gelu_exact(pre).astype(jnp.bfloat16))
                grad_pre = (cot.astype(jnp.float32) * gelu_slope(pre)).astype(jnp.bfloat16)
                if square:
                    part = gather_square(grad_pre, h == 0).reshape(-1, wide)
                else:
                    part = lax.all_gather(grad_pre, "col", axis=0, tiled=True)
                gs.append(part)
            hiddens.append(jnp.concatenate(hs, 1).reshape(blocks, sub, hidden_n))
            grads.append(jnp.concatenate(gs, 1))
        hidden = jnp.stack(hiddens, 1).reshape(owned, hidden_n)

        outs = []
        for p in range(PARTS):
            back = lax.dot_general(
                grads[p], weight, (((1,), (1,)), ((), ())), preferred_element_type=jnp.float32
            ).astype(jnp.bfloat16)
            if p == PARTS - 1:
                back, *grads = lax.optimization_barrier((back, *grads))
            outs.append(lax.psum_scatter(back, "row", scatter_dimension=0, tiled=True))
        grad_tokens = jnp.concatenate(outs, 0)
        grad_weight = dot_t(jnp.concatenate(gathered, 0), jnp.concatenate(grads, 0))
        return (hidden, grad_weight, grad_tokens)

    return shards


def solution(mesh):
    in_specs = (P("row", "col"), P("col", "row"), P("col", "row"))
    out_specs = (P("col", "row"), P("col", "row"), P("row", "col"))
    return jax.shard_map(
        make(mesh.shape["row"], mesh.shape["col"]),
        mesh=mesh,
        in_specs=in_specs,
        out_specs=out_specs,
        check_vma=False,
    )
```

time: 462 us -> 296 us (0.64)
  waiting for transfers between devices: 324 us -> 128 us
  Pallas kernels: 0 us -> 26.8 us
  local copies, waits for them, and re-layouts: 37 us -> 12.5 us
  other arithmetic: 6.57 us -> 28.9 us
  starting transfers between devices: 0.34 us -> 18.8 us
  matrix products: 80 us -> 66.7 us
    reduce_scatter x2, waiting for transfers between devices: 184 us -> 25.3 us  [shards(): outs.append(lax.psum_scatter(back, 'row', scatter_dimension=0, tiled=True))]
    all_gather x2, waiting for transfers between devices: 139 us -> 56.3 us  [shards(): lax.all_gather(tokens[p * sub:(p + 1) * sub], 'row', axis=0, tiled=True)]
    ppermute x0 -> x16, waiting for transfers between devices: none -> 45.4 us  [swap(): return lax.ppermute(value, 'col', [(c, c ^ bit) for c in range(4)])]
    unnamed x3 -> x38, local copies, waits for them, and re-layouts: 37 us -> 6.8 us
    pallas_call x0 -> x1, Pallas kernels: none -> 26.8 us  [dot_t(): pl.pallas_call(dot_t_kernel, grid=(m // block,), in_specs=[pl.BlockSpec((...]
    ppermute x0 -> x16, starting transfers between devices: none -> 18.6 us  [swap(): return lax.ppermute(value, 'col', [(c, c ^ bit) for c in range(4)])]
    concatenate x0 -> x6, other arithmetic: none -> 13.9 us  [the longest x1 6.32 us: shards(): grad_weight = dot_t(jnp.concatenate(gathered, 0), jnp.concatenate(grads, 0))]
    dot_general x3 -> x6, matrix products: 80 us -> 66.7 us  [the longest x4 35.1 us: shards(): jnp.dot(gathered[p], weight[:, cols], preferred_element_type=jnp.float32)]
  transfers between devices with their start and end apart: 4 -> 20, of which waited for: 4 -> 11; matrix products, arithmetic and copies ran while one was open for 14% -> 32% of each run, Pallas kernels for 0% -> 9%
where the time goes in v1:
time: 296 us
  waiting for transfers between devices  128 us (43%)
  matrix products  66.7 us (23%)
  other arithmetic  28.9 us (10%)
  Pallas kernels  26.8 us (9%)
  starting transfers between devices  18.8 us (6%)
  between operations  14.2 us (5%)
  local copies, waits for them, and re-layouts  12.5 us (4%)
    all_gather x2, waiting for transfers between devices, shards(): lax.all_gather(tokens[p * sub:(p + 1) * sub], 'row', axis=0, tiled=True)  56.3 us
    ppermute x16, waiting for transfers between devices, swap(): return lax.ppermute(value, 'col', [(c, c ^ bit) for c in range(4)])  45.4 us
    dot_general x4, matrix products, shards(): jnp.dot(gathered[p], weight[:, cols], preferred_element_type=jnp.float32)  35.1 us
    dot_general x2, matrix products, shards(): lax.dot_general(grads[p], weight, (((1,), (1,)), ((), ())), preferred_ele...  31.6 us
    pallas_call x1, Pallas kernels, dot_t(): pl.pallas_call(dot_t_kernel, grid=(m // block,), in_specs=[pl.BlockSpec((...  26.8 us
    reduce_scatter x2, waiting for transfers between devices, shards(): outs.append(lax.psum_scatter(back, 'row', scatter_dimension=0, tiled=True))  25.3 us
    ppermute x16, starting transfers between devices, swap(): return lax.ppermute(value, 'col', [(c, c ^ bit) for c in range(4)])  18.6 us
    unnamed x38, local copies, waits for them, and re-layouts  6.8 us
  transfers between devices with their start and end apart: 20, of which 11 were waited for; matrix products, arithmetic and copies ran while one was open for 32% of the time, Pallas kernels for 9%

profile of v1, /device:TPU:0, one launch (start us, length us, event | category | flops | bytes accessed | tf_op | source)
XLA Modules:
  0.0 295.7 jit_solution(13799272558008690338)
XLA Ops:
  7.2 2.1 fusion.41
  9.4 0.7 all-gather.3.cloned.1.call-update
  10.2 1.1 fusion.40
  11.3 39.9 %all-gather.5.cloned.1.call-done = bf16[512,3072]{1,0:T(8,128)(2,1)} async-done(((bf16[64,3072]{1,0:T(8,128)(2,1)}), bf16[512,3072]{1,0:T(8,128)(2,1)}) %all-gather.5.cloned.1.call-update) | async-done | bytes 3145744 | tf_op jit(solution)/shard_map/all_gather | solution.py:104
  51.2 9.8 %fusion = f32[512,1536]{1,0:T(8,128)S(1)} fusion(bf16[512,3072]{1,0:T(8,128)(2,1)} %all-gather.5.cloned.1.call-done, bf16[3072,3072]{1,0:T(8,128)(2,1)} %param.4), kind=kOutput, calls=%fused_computation | convolution fusion | flops 4831838208 | bytes 15728640 | tf_op jit(solution)/shard_map/dot_general | solution.py:112
  61.1 1.1 fusion.33
  62.1 1.5 collective-permute-start.6
  63.6 7.6 %fusion.4 = f32[512,1536]{1,0:T(8,128)S(1)} fusion(bf16[512,3072]{1,0:T(8,128)(2,1)S(1)} %copy-done.9, bf16[3072,3072]{1,0:T(8,128)(2,1)} %param.4), kind=kOutput, calls=%fused_computation.4 | convolution fusion | flops 4831838208 | bytes 15728640 | tf_op jit(solution)/shard_map/dot_general | solution.py:112
  71.3 1.0 fusion.35
  72.2 1.5 collective-permute-start.4
  73.7 16.4 %all-gather.3.cloned.1.call-done = bf16[512,3072]{1,0:T(8,128)(2,1)} async-done(((bf16[64,3072]{1,0:T(8,128)(2,1)}), bf16[512,3072]{1,0:T(8,128)(2,1)}) %all-gather.3.cloned.1.call-update) | async-done | bytes 3145744 | tf_op jit(solution)/shard_map/all_gather | solution.py:104
  90.1 9.9 %fusion.2 = f32[512,1536]{1,0:T(8,128)S(1)} fusion(bf16[512,3072]{1,0:T(8,128)(2,1)} %all-gather.3.cloned.1.call-done, bf16[3072,3072]{1,0:T(8,128)(2,1)} %param.4), kind=kOutput, calls=%fused_computation.2 | convolution fusion | flops 4831838208 | bytes 15728640 | tf_op jit(solution)/shard_map/dot_general | solution.py:112
  100.0 1.5 collective-permute-start.2
  101.6 7.8 %fusion.6 = f32[512,1536]{1,0:T(8,128)S(1)} fusion(bf16[512,3072]{1,0:T(8,128)(2,1)S(1)} %copy-done.11, bf16[3072,3072]{1,0:T(8,128)(2,1)} %param.4), kind=kOutput, calls=%fused_computation.6 | convolution fusion | flops 4831838208 | bytes 15728640 | tf_op jit(solution)/shard_map/dot_general | solution.py:112
  109.5 1.5 collective-permute-start
  111.0 1.3 bitcast_add_fusion
  112.4 0.6 collective-permute-start.7
  113.1 1.3 bitcast_add_fusion.1
  114.4 0.9 collective-permute-start.5
  115.4 5.1 %collective-permute-done.2 = bf16[2,128,1536]{2,1,0:T(8,128)(2,1)S(1)} collective-permute-done((bf16[2,128,1536]{2,1,0:T(8,128)(2,1)S(1)}, bf16[2,128,1536]{2,1,0:T(8,128)(2,1)S(1)}, u32[]{:S(2)}, u32[]{:S(2)}) %collective-permute-start.2) | collective-permute-done | bytes 786464 | tf_op jit(solution)/shard_map/ppermute | solution.py:51
  120.8 1.5 collective-permute-start.3
  122.3 7.7 %collective-permute-done = bf16[2,128,1536]{2,1,0:T(8,128)(2,1)S(1)} collective-permute-done((bf16[2,128,1536]{2,1,0:T(8,128)(2,1)S(1)}, bf16[2,128,1536]{2,1,0:T(8,128)(2,1)S(1)}, u32[]{:S(2)}, u32[]{:S(2)}) %collective-permute-start) | collective-permute-done | bytes 786464 | tf_op jit(solution)/shard_map/ppermute | solution.py:51
  130.2 0.9 collective-permute-start.1
  131.2 7.2 %collective-permute-done.7 = bf16[128,1536]{1,0:T(8,128)(2,1)S(1)} collective-permute-done((bf16[128,1536]{1,0:T(8,128)(2,1)S(1)}, bf16[128,1536]{1,0:T(8,128)(2,1)S(1)}, u32[]{:S(2)}, u32[]{:S(2)}) %collective-permute-start.7) | collective-permute-done | bytes 393248 | tf_op jit(solution)/shard_map/ppermute | solution.py:51
  138.4 1.2 fusion.19
  139.6 0.9 collective-permute-start.10
  140.5 1.3 fusion.13
  141.8 1.5 collective-permute-start.8
  143.2 3.6 %collective-permute-done.3 = bf16[128,1536]{1,0:T(8,128)(2,1)S(1)} collective-permute-done((bf16[128,1536]{1,0:T(8,128)(2,1)S(1)}, bf16[128,1536]{1,0:T(8,128)(2,1)S(1)}, u32[]{:S(2)}, u32[]{:S(2)}) %collective-permute-start.3) | collective-permute-done | bytes 393248 | tf_op jit(solution)/shard_map/ppermute | solution.py:51
  146.8 1.2 fusion.31
  148.1 0.9 collective-permute-start.14
  148.9 1.2 fusion.25
  150.2 1.5 collective-permute-start.12
  151.8 0.6 collective-permute-start.11
  152.4 2.8 collective-permute-done.8
  155.4 0.9 collective-permute-start.9
  156.4 1.7 collective-permute-done.14
  158.1 0.9 pad_maximum_fusion.14
  159.1 1.5 collective-permute-start.15
  160.6 3.1 %collective-permute-done.12 = bf16[128,1536]{1,0:T(8,128)(2,1)S(1)} collective-permute-done((bf16[128,1536]{1,0:T(8,128)(2,1)S(1)}, bf16[128,1536]{1,0:T(8,128)(2,1)S(1)}, u32[]{:S(2)}, u32[]{:S(2)}) %collective-permute-start.12) | collective-permute-done | bytes 393248 | tf_op jit(solution)/shard_map/ppermute | solution.py:51
  163.7 0.8 copy-done.7
  164.5 1.0 pad_maximum_fusion.13
  165.5 0.9 collective-permute-start.13
  166.3 14.2 %collective-permute-done.11 = bf16[2,128,1536]{2,1,0:T(8,128)(2,1)S(1)} collective-permute-done((bf16[2,128,1536]{2,1,0:T(8,128)(2,1)S(1)}, bf16[2,128,1536]{2,1,0:T(8,128)(2,1)S(1)}, u32[]{:S(2)}, u32[]{:S(2)}) %collective-permute-start.11) | collective-permute-done | bytes 786464 | tf_op jit(solution)/shard_map/ppermute | solution.py:51
  181.1 0.8 copy-done.1
  181.9 0.5 copy-done.4
  182.5 15.2 %convolution_convert_fusion.1 = bf16[512,3072]{1,0:T(8,128)(2,1)} fusion(bf16[3072,3072]{1,0:T(8,128)(2,1)} %param.4, bf16[512,1536]{1,0:T(8,128)(2,1)S(1)} %bitcast.148, bf16[512,1536]{1,0:T(8,128)(2,1)S(1)} %bitcast.152), kind=kOutput, calls=%fused_computation.11 | convolution fusion | flops 9671540736 | bytes 25165824 | tf_op jit(solution)/shard_map/dot_general | solution.py:133
  197.7 1.2 select_bitcast_fusion.1
  199.2 1.1 copy-done.2
  200.3 0.5 copy-done.5
  200.8 0.4 pad_maximum_fusion.2
  201.2 0.9 copy-done.8
  202.1 1.3 select_bitcast_fusion.3
  203.5 1.2 copy-done.6
  204.7 2.0 pad_maximum_fusion.3
  206.8 16.4 %convolution_convert_fusion = bf16[512,3072]{1,0:T(8,128)(2,1)} fusion(bf16[3072,3072]{1,0:T(8,128)(2,1)} %param.4, bf16[512,1536]{1,0:T(8,128)(2,1)} %bitcast.151, bf16[512,1536]{1,0:T(8,128)(2,1)} %bitcast.155), kind=kOutput, calls=%fused_computation.10 | convolution fusion | flops 9671540736 | bytes 25165824 | tf_op jit(solution)/shard_map/dot_general | solution.py:133
  223.2 1.0 copy-done.18
  224.2 1.2 pad_maximum_fusion.10
  225.4 1.9 pad_maximum_fusion.9
  227.4 1.3 pad_maximum_fusion.4
  228.7 6.3 %pad_maximum_fusion = (bf16[1024,3072]{1,0:T(8,128)(2,1)}, bf16[1024,3072]{1,0:T(8,128)(2,1)}) fusion(bf16[512,3072]{1,0:T(8,128)(2,1)S(1)} %copy-done.10, bf16[512,3072]{1,0:T(8,128)(2,1)} %all-gather.3.cloned.1.call-done, bf16[512,3072]{1,0:T(8,128)(2,1)S(1)} %pad_maximum_fusion.2, bf16[512,3072]{1,0:T(8,128)(2,1)S(1)} %copy-done), kind=kLoop, calls=%fused_computation.8 | loop fusion | flops 25165824 | bytes 25165824 | tf_op jit(solution)/shard_map/concatenate | solution.py:140
  235.0 26.8 %shard_map.58 = f32[3072,3072]{1,0:T(8,128)} custom-call(bf16[1024,3072]{1,0:T(8,128)(2,1)} %get-tuple-element.39.a_ref, bf16[1024,3072]{1,0:T(8,128)(2,1)} %get-tuple-element.40.b_ref), custom_call_target="tpu_custom_call" | custom-call | flops 19327352832 | bytes 50331648 | tf_op jit(solution)/shard_map/pallas_call | solution.py:32
  261.8 25.3 %reduce-scatter.3.cloned.1.call-done = bf16[64,3072]{1,0:T(8,128)(2,1)} async-done(((bf16[512,3072]{1,0:T(8,128)(2,1)}), bf16[64,3072]{1,0:T(8,128)(2,1)}) %reduce-scatter.3.cloned.1.call-update) | async-done | bytes 393232 | tf_op jit(solution)/shard_map/reduce_scatter | solution.py:138
  287.1 2.0 pad_maximum_fusion.15
  (67 shorter events, 2.4 us)
Async XLA Ops:
  7.2 3.1 %copy-start.17 = (bf16[256,3072]{1,0:T(8,128)(2,1)S(1)}, bf16[256,3072]{1,0:T(8,128)(2,1)}, u32[]{:S(2)}) copy-start(bf16[256,3072]{1,0:T(8,128)(2,1)} %param.5) | copy-start | bytes 4718596
  7.2 44.1 %all-gather.5.cloned.1.call-start = ((), (), s32[]{:S(2)}) async-start(), calls=%async_computation.3 | async-start | bytes 3538944 | tf_op jit(solution)/shard_map/all_gather | solution.py:104
  9.4 80.7 %all-gather.3.cloned.1.call-start = ((), (), s32[]{:S(2)}) async-start(), calls=%async_computation.2 | async-start | bytes 3538944 | tf_op jit(solution)/shard_map/all_gather | solution.py:104
  10.1 251.7 %reduce-scatter.5.cloned.1.call-start = ((), (), s32[]{:S(2)}) async-start(), calls=%async_computation.5 | async-start | bytes 3538944 | tf_op jit(solution)/shard_map/reduce_scatter | solution.py:138
  51.2 12.4 %copy-start.9 = (bf16[512,3072]{1,0:T(8,128)(2,1)S(1)}, bf16[512,3072]{1,0:T(8,128)(2,1)}, u32[]{:S(2)}) copy-start(bf16[512,3072]{1,0:T(8,128)(2,1)} %all-gather.5.cloned.1.call-done) | copy-start | bytes 9437188
  61.1 10.2 %copy-start.12 = (f32[512,1536]{1,0:T(8,128)}, f32[512,1536]{1,0:T(8,128)S(1)}, u32[]{:S(2)}) copy-start(f32[512,1536]{1,0:T(8,128)S(1)} %fusion) | copy-start | bytes 9437188
  62.1 48.9 %collective-permute-start.6 = (bf16[2,128,1536]{2,1,0:T(8,128)(2,1)}, bf16[2,128,1536]{2,1,0:T(8,128)(2,1)}, u32[]{:S(2)}, u32[]{:S(2)}) collective-permute-start(bf16[2,128,1536]{2,1,0:T(8,128)(2,1)} %fusion.33), channel_id=1, source_target_pairs={{0,2},{1,3},{2,0},{3,1},{4,6},{5,7},{6,4},{7,5},{8,10},{9,11},{10,... | collective-permute-start | bytes 2359304 | tf_op jit(solution)/shard_map/ppermute | solution.py:51
  72.2 40.8 %collective-permute-start.4 = (bf16[2,128,1536]{2,1,0:T(8,128)(2,1)}, bf16[2,128,1536]{2,1,0:T(8,128)(2,1)}, u32[]{:S(2)}, u32[]{:S(2)}) collective-permute-start(bf16[2,128,1536]{2,1,0:T(8,128)(2,1)} %fusion.35), channel_id=1, source_target_pairs={{0,1},{1,0},{2,3},{3,2},{4,5},{5,4},{6,7},{7,6},{8,9},{9,8},{10,11... | collective-permute-start | bytes 2359304 | tf_op jit(solution)/shard_map/ppermute | solution.py:51
  90.1 11.5 %copy-start.11 = (bf16[512,3072]{1,0:T(8,128)(2,1)S(1)}, bf16[512,3072]{1,0:T(8,128)(2,1)}, u32[]{:S(2)}) copy-start(bf16[512,3072]{1,0:T(8,128)(2,1)} %all-gather.3.cloned.1.call-done) | copy-start | bytes 9437188
  100.0 11.0 %copy-start.13 = (f32[512,1536]{1,0:T(8,128)S(1)}, f32[512,1536]{1,0:T(8,128)}, u32[]{:S(2)}) copy-start(f32[512,1536]{1,0:T(8,128)} %copy-done.12) | copy-start | bytes 9437188
  100.0 20.4 %collective-permute-start.2 = (bf16[2,128,1536]{2,1,0:T(8,128)(2,1)S(1)}, bf16[2,128,1536]{2,1,0:T(8,128)(2,1)S(1)}, u32[]{:S(2)}, u32[]{:S(2)}) collective-permute-start(bf16[2,128,1536]{2,1,0:T(8,128)(2,1)S(1)} %fusion.32), channel_id=1, source_target_pairs={{0,2},{1,3},{2,0},{3,1},{4,6},{5,7},{6,4},{7,5},{8,10},{9,11},{10,... | collective-permute-start | bytes 2359304 | tf_op jit(solution)/shard_map/ppermute | solution.py:51
  109.5 20.5 %collective-permute-start = (bf16[2,128,1536]{2,1,0:T(8,128)(2,1)S(1)}, bf16[2,128,1536]{2,1,0:T(8,128)(2,1)S(1)}, u32[]{:S(2)}, u32[]{:S(2)}) collective-permute-start(bf16[2,128,1536]{2,1,0:T(8,128)(2,1)S(1)} %fusion.34), channel_id=1, source_target_pairs={{0,1},{1,0},{2,3},{3,2},{4,5},{5,4},{6,7},{7,6},{8,9},{9,8},{10,11... | collective-permute-start | bytes 2359304 | tf_op jit(solution)/shard_map/ppermute | solution.py:51
  112.4 26.0 %collective-permute-start.7 = (bf16[128,1536]{1,0:T(8,128)(2,1)S(1)}, bf16[128,1536]{1,0:T(8,128)(2,1)S(1)}, u32[]{:S(2)}, u32[]{:S(2)}) collective-permute-start(bf16[128,1536]{1,0:T(8,128)(2,1)S(1)} %fusion.39), channel_id=1, source_target_pairs={{0,1},{1,0},{2,3},{3,2},{4,5},{5,4},{6,7},{7,6},{8,9},{9,8},{10,11... | collective-permute-start | bytes 1179656 | tf_op jit(solution)/shard_map/ppermute | solution.py:51
  114.4 26.1 %collective-permute-start.5 = (bf16[128,1536]{1,0:T(8,128)(2,1)S(1)}, bf16[128,1536]{1,0:T(8,128)(2,1)S(1)}, u32[]{:S(2)}, u32[]{:S(2)}) collective-permute-start(bf16[128,1536]{1,0:T(8,128)(2,1)S(1)} %fusion.38), channel_id=1, source_target_pairs={{0,2},{1,3},{2,0},{3,1},{4,6},{5,7},{6,4},{7,5},{8,10},{9,11},{10,... | collective-permute-start | bytes 1179656 | tf_op jit(solution)/shard_map/ppermute | solution.py:51
  120.7 17.7 %copy-start.16 = (bf16[2,1,64,1536]{3,2,1,0:T(8,128)(2,1)S(1)}, bf16[2,1,64,1536]{3,2,1,0:T(8,128)(2,1)}, u32[]{:S(2)}) copy-start(bf16[2,1,64,1536]{3,2,1,0:T(8,128)(2,1)} %get-tuple-element.21) | copy-start | bytes 1179652
  120.7 19.8 %copy-start.15 = (bf16[2,1,64,1536]{3,2,1,0:T(8,128)(2,1)S(1)}, bf16[2,1,64,1536]{3,2,1,0:T(8,128)(2,1)}, u32[]{:S(2)}) copy-start(bf16[2,1,64,1536]{3,2,1,0:T(8,128)(2,1)} %get-tuple-element.22) | copy-start | bytes 1179652
  120.8 26.1 %collective-permute-start.3 = (bf16[128,1536]{1,0:T(8,128)(2,1)S(1)}, bf16[128,1536]{1,0:T(8,128)(2,1)S(1)}, u32[]{:S(2)}, u32[]{:S(2)}) collective-permute-start(bf16[128,1536]{1,0:T(8,128)(2,1)S(1)} %fusion.37), channel_id=1, source_target_pairs={{0,1},{1,0},{2,3},{3,2},{4,5},{5,4},{6,7},{7,6},{8,9},{9,8},{10,11... | collective-permute-start | bytes 1179656 | tf_op jit(solution)/shard_map/ppermute | solution.py:51
  130.2 16.7 %copy-start.14 = (bf16[2,1,64,1536]{3,2,1,0:T(8,128)(2,1)S(1)}, bf16[2,1,64,1536]{3,2,1,0:T(8,128)(2,1)}, u32[]{:S(2)}) copy-start(bf16[2,1,64,1536]{3,2,1,0:T(8,128)(2,1)} %get-tuple-element.20) | copy-start | bytes 1179652
  130.2 18.7 %collective-permute-start.1 = (bf16[128,1536]{1,0:T(8,128)(2,1)S(1)}, bf16[128,1536]{1,0:T(8,128)(2,1)S(1)}, u32[]{:S(2)}, u32[]{:S(2)}) collective-permute-start(bf16[128,1536]{1,0:T(8,128)(2,1)S(1)} %fusion.36), channel_id=1, source_target_pairs={{0,2},{1,3},{2,0},{3,1},{4,6},{5,7},{6,4},{7,5},{8,10},{9,11},{10,... | collective-permute-start | bytes 1179656 | tf_op jit(solution)/shard_map/ppermute | solution.py:51
  139.6 12.0 %collective-permute-start.10 = (bf16[128,1536]{1,0:T(8,128)(2,1)S(1)}, bf16[128,1536]{1,0:T(8,128)(2,1)S(1)}, u32[]{:S(2)}, u32[]{:S(2)}) collective-permute-start(bf16[128,1536]{1,0:T(8,128)(2,1)S(1)} %get-tuple-element.15), channel_id=1, source_target_pairs={{0,2},{1,3},{2,0},{3,1},{4,6},{5,7},{6,4},{7,5},{8,10},{9,11},{10,... | collective-permute-start | bytes 1179656 | tf_op jit(solution)/shard_map/ppermute | solution.py:51
  141.8 13.5 %collective-permute-start.8 = (bf16[128,1536]{1,0:T(8,128)(2,1)S(1)}, bf16[128,1536]{1,0:T(8,128)(2,1)S(1)}, u32[]{:S(2)}, u32[]{:S(2)}) collective-permute-start(bf16[128,1536]{1,0:T(8,128)(2,1)S(1)} %get-tuple-element.13), channel_id=1, source_target_pairs={{0,1},{1,0},{2,3},{3,2},{4,5},{5,4},{6,7},{7,6},{8,9},{9,8},{10,11... | collective-permute-start | bytes 1179656 | tf_op jit(solution)/shard_map/ppermute | solution.py:51
  148.1 10.0 %collective-permute-start.14 = (bf16[128,1536]{1,0:T(8,128)(2,1)S(1)}, bf16[128,1536]{1,0:T(8,128)(2,1)S(1)}, u32[]{:S(2)}, u32[]{:S(2)}) collective-permute-start(bf16[128,1536]{1,0:T(8,128)(2,1)S(1)} %get-tuple-element.11), channel_id=1, source_target_pairs={{0,2},{1,3},{2,0},{3,1},{4,6},{5,7},{6,4},{7,5},{8,10},{9,11},{10,... | collective-permute-start | bytes 1179656 | tf_op jit(solution)/shard_map/ppermute | solution.py:51
  150.2 13.5 %collective-permute-start.12 = (bf16[128,1536]{1,0:T(8,128)(2,1)S(1)}, bf16[128,1536]{1,0:T(8,128)(2,1)S(1)}, u32[]{:S(2)}, u32[]{:S(2)}) collective-permute-start(bf16[128,1536]{1,0:T(8,128)(2,1)S(1)} %get-tuple-element.9), channel_id=1, source_target_pairs={{0,1},{1,0},{2,3},{3,2},{4,5},{5,4},{6,7},{7,6},{8,9},{9,8},{10,11... | collective-permute-start | bytes 1179656 | tf_op jit(solution)/shard_map/ppermute | solution.py:51
  151.8 28.7 %collective-permute-start.11 = (bf16[2,128,1536]{2,1,0:T(8,128)(2,1)S(1)}, bf16[2,128,1536]{2,1,0:T(8,128)(2,1)S(1)}, u32[]{:S(2)}, u32[]{:S(2)}) collective-permute-start(bf16[2,128,1536]{2,1,0:T(8,128)(2,1)S(1)} %pad_maximum_fusion.12), channel_id=1, source_target_pairs={{0,1},{1,0},{2,3},{3,2},{4,5},{5,4},{6,7},{7,6},{8,9},{9,8},{10,11... | collective-permute-start | bytes 2359304 | tf_op jit(solution)/shard_map/ppermute | solution.py:51
  155.4 25.4 %collective-permute-start.9 = (bf16[2,128,1536]{2,1,0:T(8,128)(2,1)S(1)}, bf16[2,128,1536]{2,1,0:T(8,128)(2,1)S(1)}, u32[]{:S(2)}, u32[]{:S(2)}) collective-permute-start(bf16[2,128,1536]{2,1,0:T(8,128)(2,1)S(1)} %pad_maximum_fusion.11), channel_id=1, source_target_pairs={{0,2},{1,3},{2,0},{3,1},{4,6},{5,7},{6,4},{7,5},{8,10},{9,11},{10,... | collective-permute-start | bytes 2359304 | tf_op jit(solution)/shard_map/ppermute | solution.py:51
  159.1 38.6 %collective-permute-start.15 = (bf16[2,128,1536]{2,1,0:T(8,128)(2,1)}, bf16[2,128,1536]{2,1,0:T(8,128)(2,1)}, u32[]{:S(2)}, u32[]{:S(2)}) collective-permute-start(bf16[2,128,1536]{2,1,0:T(8,128)(2,1)} %pad_maximum_fusion.14), channel_id=1, source_target_pairs={{0,1},{1,0},{2,3},{3,2},{4,5},{5,4},{6,7},{7,6},{8,9},{9,8},{10,11... | collective-permute-start | bytes 2359304 | tf_op jit(solution)/shard_map/ppermute | solution.py:51
  163.7 0.8 copy-start.7
  165.5 35.7 %collective-permute-start.13 = (bf16[2,128,1536]{2,1,0:T(8,128)(2,1)}, bf16[2,128,1536]{2,1,0:T(8,128)(2,1)}, u32[]{:S(2)}, u32[]{:S(2)}) collective-permute-start(bf16[2,128,1536]{2,1,0:T(8,128)(2,1)} %pad_maximum_fusion.13), channel_id=1, source_target_pairs={{0,2},{1,3},{2,0},{3,1},{4,6},{5,7},{6,4},{7,5},{8,10},{9,11},{10,... | collective-permute-start | bytes 2359304 | tf_op jit(solution)/shard_map/ppermute | solution.py:51
  180.8 1.1 copy-start.1
  181.1 1.4 copy-start.4
  198.9 1.4 copy-start.2
  198.9 1.9 copy-start.5
  200.8 2.7 copy-start.3
  200.8 1.3 copy-start.8
  203.5 1.2 copy-start.6
  206.8 80.4 %reduce-scatter.3.cloned.1.call-start = ((), (), s32[]{:S(2)}) async-start(), calls=%async_computation.4 | async-start | bytes 3538944 | tf_op jit(solution)/shard_map/reduce_scatter | solution.py:138
  223.2 1.0 copy-start.18
  224.2 4.5 %copy-start = (bf16[512,3072]{1,0:T(8,128)(2,1)S(1)}, bf16[512,3072]{1,0:T(8,128)(2,1)}, u32[]{:S(2)}) copy-start(bf16[512,3072]{1,0:T(8,128)(2,1)} %pad_maximum_fusion.3) | copy-start | bytes 9437188
  224.2 4.5 %copy-start.10 = (bf16[512,3072]{1,0:T(8,128)(2,1)S(1)}, bf16[512,3072]{1,0:T(8,128)(2,1)}, u32[]{:S(2)}) copy-start(bf16[512,3072]{1,0:T(8,128)(2,1)} %all-gather.5.cloned.1.call-done) | copy-start | bytes 9437188
Sparse Core Ops, SparseCore 0:
  10.2 40.9 all-gather.4
  52.9 37.1 all-gather.2
  206.9 38.5 reduce-scatter.4
  247.7 39.4 reduce-scatter.2

commit v2 on v1

v2 whole, which is shorter than its diff:
```python
import math

import jax
import jax.numpy as jnp
from jax import lax
from jax.experimental import pallas as pl
from jax.experimental.pallas import tpu as pltpu
from jax.sharding import PartitionSpec as P

PARTS = 4


def gelu_exact(value):
    return 0.5 * value * (1.0 + jax.scipy.special.erf(value / math.sqrt(2.0)))


def gelu_slope(value):
    cumulative = 0.5 * (1.0 + jax.scipy.special.erf(value / math.sqrt(2.0)))
    return cumulative + value * jnp.exp(-0.5 * value * value) / math.sqrt(2.0 * math.pi)


def dot_parts_kernel(a_ref, *refs):
    parts, out_ref, held = refs[:-2], refs[-2], refs[-1]
    rows = parts[0].shape[0]

    @pl.when(pl.program_id(0) == 0)
    def _():
        for p, part in enumerate(parts):
            held[p * rows : (p + 1) * rows] = part[...]

    out_ref[...] = jnp.dot(a_ref[...], held[...], preferred_element_type=jnp.float32)


def dot_parts(a, parts):
    m, depth = a.shape
    rows, n = parts[0].shape
    block = 256
    return pl.pallas_call(
        dot_parts_kernel,
        grid=(m // block,),
        in_specs=[pl.BlockSpec((block, depth), lambda i: (i, 0))]
        + [pl.BlockSpec((rows, n), lambda i: (0, 0)) for _ in parts],
        out_specs=pl.BlockSpec((block, n), lambda i: (i, 0)),
        out_shape=jax.ShapeDtypeStruct((m, n), jnp.float32),
        scratch_shapes=[pltpu.VMEM((depth, n), jnp.bfloat16)],
        compiler_params=pltpu.CompilerParams(vmem_limit_bytes=48 * 1024 * 1024),
        cost_estimate=pl.CostEstimate(
            flops=2 * depth * m * n,
            bytes_accessed=2 * depth * (m + n) + 4 * m * n,
            transcendentals=0,
        ),
    )(a, *parts)


def swap(value, bit):
    return lax.ppermute(value, "col", [(c, c ^ bit) for c in range(4)])


def pick(value, axis, index):
    return lax.dynamic_index_in_dim(value, index, axis, keepdims=False)


def ordered(mine, other, index, axis):
    first = jnp.where(index == 0, mine, other)
    second = jnp.where(index == 0, other, mine)
    return jnp.stack([first, second], axis)


def scatter_first(partial, x_first):
    me = lax.axis_index("col")
    x, y = me % 2, me // 2
    a = partial.reshape((2, 2) + partial.shape[1:])
    axis, bit, at = (1, 1, x) if x_first else (0, 2, y)
    got = swap(pick(a, axis, 1 - at).astype(jnp.bfloat16), bit)
    return pick(a, axis, at) + got.astype(jnp.float32)


def scatter_second(a, x_first):
    me = lax.axis_index("col")
    bit, at = (2, me // 2) if x_first else (1, me % 2)
    got = swap(pick(a, 0, 1 - at).astype(jnp.bfloat16), bit)
    return pick(a, 0, at) + got.astype(jnp.float32)


def pair_sum(partial, n):
    core = lax.axis_index("row") % 2
    a = partial.reshape((n // 2, 2) + partial.shape[1:])
    got = lax.ppermute(
        pick(a, 1, 1 - core).astype(jnp.bfloat16), "row", [(r, r ^ 1) for r in range(n)]
    )
    return pick(a, 1, core) + got.astype(jnp.float32)


def scatter_z(a, n):
    z, nz = lax.axis_index("row") // 2, n // 2
    total = pick(a, 0, z)
    for k in range(1, nz):
        block = pick(a, 0, (z + k) % nz).astype(jnp.bfloat16)
        got = lax.ppermute(block, "row", [(r, (r + 2 * k) % n) for r in range(n)])
        total = total + got.astype(jnp.float32)
    return total.astype(jnp.bfloat16)


def gather_square(value, x_first):
    me = lax.axis_index("col")
    x, y = me % 2, me // 2
    if x_first:
        pair = ordered(value, swap(value, 1), x, 0)
        both = ordered(pair, swap(pair, 2), y, 0)
    else:
        pair = ordered(value, swap(value, 2), y, 0)
        both = ordered(pair, swap(pair, 1), x, 1)
    return both.reshape((4,) + value.shape)


def make(row_n, col_n):
    def shards(tokens, weight, cotangent):
        local, features = tokens.shape
        hidden_n = weight.shape[1]
        owned = cotangent.shape[0]
        sub = local // PARTS
        blocks = owned // local
        square = col_n == 4
        cuts = 2 if square else 1
        wide = hidden_n // cuts
        split = cotangent.reshape(blocks, PARTS, sub, hidden_n)

        gathered = [
            lax.all_gather(tokens[p * sub : (p + 1) * sub], "row", axis=0, tiled=True)
            for p in range(PARTS)
        ]
        hiddens, grads, outs = [], [], []
        for p in range(PARTS):
            rows, firsts = gathered[p], []
            if square and p:
                rows, *_ = lax.optimization_barrier((rows, *held))
            for h in range(cuts):
                cols = slice(h * wide, (h + 1) * wide)
                partial = jnp.dot(rows, weight[:, cols], preferred_element_type=jnp.float32)
                if square:
                    partial = partial.reshape(col_n, blocks * sub, wide)
                    firsts.append(scatter_first(partial, h == 0))
                else:
                    firsts.append(partial)
            held = firsts
            hs, gs = [], []
            for h in range(cuts):
                cols = slice(h * wide, (h + 1) * wide)
                if square:
                    pre = scatter_second(firsts[h], h == 0)
                else:
                    pre = lax.psum_scatter(firsts[h], "col", scatter_dimension=0, tiled=True)
                cot = split[:, p, :, cols].reshape(blocks * sub, wide)
                hs.append(gelu_exact(pre).astype(jnp.bfloat16))
                grad_pre = (cot.astype(jnp.float32) * gelu_slope(pre)).astype(jnp.bfloat16)
                if square:
                    part = gather_square(grad_pre, h == 0).reshape(-1, wide)
                else:
                    part = lax.all_gather(grad_pre, "col", axis=0, tiled=True)
                gs.append(part)
            hiddens.append(jnp.concatenate(hs, 1).reshape(blocks, sub, hidden_n))
            grad = jnp.concatenate(gs, 1)
            if p:
                grad, _ = lax.optimization_barrier((grad, pairs))
            back = lax.dot_general(
                grad, weight, (((1,), (1,)), ((), ())), preferred_element_type=jnp.float32
            )
            grads.append(grad)
            pairs = pair_sum(back.reshape(row_n, sub, features), row_n)
            if p == PARTS - 1:
                pairs, *grads = lax.optimization_barrier((pairs, *grads))
            outs.append(scatter_z(pairs, row_n))
        hidden = jnp.stack(hiddens, 1).reshape(owned, hidden_n)
        grad_tokens = jnp.concatenate(outs, 0)
        *gathered, _ = lax.optimization_barrier((*gathered, held[0]))
        turned = jnp.concatenate(gathered, 0).T
        grad_weight = dot_parts(turned, grads)
        return (hidden, grad_weight, grad_tokens)

    return shards


def solution(mesh):
    in_specs = (P("row", "col"), P("col", "row"), P("col", "row"))
    out_specs = (P("col", "row"), P("col", "row"), P("row", "col"))
    return jax.shard_map(
        make(mesh.shape["row"], mesh.shape["col"]),
        mesh=mesh,
        in_specs=in_specs,
        out_specs=out_specs,
        check_vma=False,
    )
```

time: 296 us -> 324 us (1.095)
  waiting for transfers between devices: 128 us -> 79.6 us
  starting transfers between devices: 18.8 us -> 52.5 us
  matrix products: 66.7 us -> 84.5 us
  local copies, waits for them, and re-layouts: 12.5 us -> 27.2 us
  other arithmetic: 28.9 us -> 38.8 us
    all_gather x2 -> x4, waiting for transfers between devices: 56.3 us -> 27.1 us  [shards(): lax.all_gather(tokens[p * sub:(p + 1) * sub], 'row', axis=0, tiled=True)]
    reduce_scatter x2 -> x0, waiting for transfers between devices: 25.3 us -> none  [shards(): outs.append(lax.psum_scatter(back, 'row', scatter_dimension=0, tiled=True))]
    ppermute x0 -> x16, waiting for transfers between devices: none -> 22.1 us  [the longest x12 22.1 us: scatter_z(): got = lax.ppermute(block, 'row', [(r, (r + 2 * k) % n) for r in range(n)])]
    dot_general x6 -> x12, matrix products: 66.7 us -> 84.5 us  [the longest x8 48.2 us: shards(): partial = jnp.dot(rows, weight[:, cols], preferred_element_type=jnp.float32)]
    ppermute x16 -> x32, waiting for transfers between devices: 45.4 us -> 28.5 us  [swap(): return lax.ppermute(value, 'col', [(c, c ^ bit) for c in range(4)])]
    ppermute x16 -> x32, starting transfers between devices: 18.6 us -> 35.6 us  [swap(): return lax.ppermute(value, 'col', [(c, c ^ bit) for c in range(4)])]
    ppermute x0 -> x16, starting transfers between devices: none -> 16.8 us  [the longest x12 16.6 us: scatter_z(): got = lax.ppermute(block, 'row', [(r, (r + 2 * k) % n) for r in range(n)])]
    another operation x16 -> x32, other arithmetic: 5.66 us -> 18.6 us  [ordered(): return jnp.stack([first, second], axis)]
  transfers between devices with their start and end apart: 20 -> 52, of which waited for: 11 -> 13; matrix products, arithmetic and copies ran while one was open for 32% -> 41% of each run, Pallas kernels for 9% -> 8%
where the time goes in v2:
time: 324 us; the launch traced here: 323 us
  matrix products  84.5 us (26%)
  waiting for transfers between devices  79.6 us (25%)
  starting transfers between devices  52.5 us (16%)
  other arithmetic  38.8 us (12%)
  local copies, waits for them, and re-layouts  27.2 us (8%)
  Pallas kernels  25.4 us (8%)
  between operations  14.9 us (5%)
    dot_general x8, matrix products, shards(): partial = jnp.dot(rows, weight[:, cols], preferred_element_type=jnp.float32)  48.2 us
    dot_general x4, matrix products, shards(): lax.dot_general(grad, weight, (((1,), (1,)), ((), ())), preferred_element...  36.3 us
    ppermute x32, starting transfers between devices, swap(): return lax.ppermute(value, 'col', [(c, c ^ bit) for c in range(4)])  35.6 us
    ppermute x32, waiting for transfers between devices, swap(): return lax.ppermute(value, 'col', [(c, c ^ bit) for c in range(4)])  28.5 us
    all_gather x4, waiting for transfers between devices, shards(): lax.all_gather(tokens[p * sub:(p + 1) * sub], 'row', axis=0, tiled=True)  27.1 us
    pallas_call x1, Pallas kernels, dot_parts(): pl.pallas_call(dot_parts_kernel, grid=(m // block,), in_specs=[pl.BlockSp...  25.4 us
    ppermute x12, waiting for transfers between devices, scatter_z(): got = lax.ppermute(block, 'row', [(r, (r + 2 * k) % n) for r in range(n)])  22.1 us
    another operation x32, other arithmetic, ordered(): return jnp.stack([first, second], axis)  18.6 us
  transfers between devices with their start and end apart: 52, of which 13 were waited for; matrix products, arithmetic and copies ran while one was open for 41% of the time, Pallas kernels for 8%

profile of v2, /device:TPU:0, one launch (start us, length us, event | category | flops | bytes accessed | tf_op | source)
XLA Modules:
  0.0 323.0 jit_solution(3507247853078298877)
XLA Ops:
  7.2 2.2 fusion.110
  12.7 25.4 %all-gather.5.cloned.1.call-done = bf16[256,3072]{1,0:T(8,128)(2,1)} async-done(((bf16[32,3072]{1,0:T(8,128)(2,1)}), bf16[256,3072]{1,0:T(8,128)(2,1)}) %all-gather.5.cloned.1.call-update) | async-done | bytes 1572880 | tf_op jit(solution)/shard_map/all_gather | solution.py:129
  38.0 6.8 %fusion.6 = f32[256,1536]{1,0:T(8,128)S(1)} fusion(bf16[256,3072]{1,0:T(8,128)(2,1)} %all-gather.5.cloned.1.call-done, bf16[3072,3072]{1,0:T(8,128)(2,1)} %param.4), kind=kOutput, calls=%fused_computation.7 | convolution fusion | flops 2415919104 | bytes 12582912 | tf_op jit(solution)/shard_map/dot_general | solution.py:139
  44.9 1.5 collective-permute-start.2
  46.5 5.4 %fusion.14 = f32[256,1536]{1,0:T(8,128)S(1)} fusion(bf16[256,3072]{1,0:T(8,128)(2,1)S(1)} %copy-done.22, bf16[3072,3072]{1,0:T(8,128)(2,1)} %param.4), kind=kOutput, calls=%fused_computation.15 | convolution fusion | flops 2415919104 | bytes 12582912 | tf_op jit(solution)/shard_map/dot_general | solution.py:139
  51.9 1.6 collective-permute-start
  53.5 2.7 collective-permute-done.2
  56.4 6.6 %collective-permute-done = bf16[2,64,1536]{2,1,0:T(8,128)(2,1)S(1)} collective-permute-done((bf16[2,64,1536]{2,1,0:T(8,128)(2,1)S(1)}, bf16[2,64,1536]{2,1,0:T(8,128)(2,1)S(1)}, u32[]{:S(2)}, u32[]{:S(2)}) %collective-permute-start) | collective-permute-done | bytes 393248 | tf_op jit(solution)/shard_map/ppermute | solution.py:56
  63.1 1.7 all-gather.7.cloned.1.call-done
  64.8 7.0 %fusion.4 = f32[256,1536]{1,0:T(8,128)S(1)} fusion(bf16[256,3072]{1,0:T(8,128)(2,1)} %all-gather.7.cloned.1.call-done, bf16[3072,3072]{1,0:T(8,128)(2,1)} %param.4), kind=kOutput, calls=%fused_computation.5 | convolution fusion | flops 2415919104 | bytes 12582912 | tf_op jit(solution)/shard_map/dot_general | solution.py:139
  71.9 5.5 %fusion.12 = f32[256,1536]{1,0:T(8,128)S(1)} fusion(bf16[256,3072]{1,0:T(8,128)(2,1)S(1)} %copy-done.23, bf16[3072,3072]{1,0:T(8,128)(2,1)} %param.4), kind=kOutput, calls=%fused_computation.13 | convolution fusion | flops 2415919104 | bytes 12582912 | tf_op jit(solution)/shard_map/dot_general | solution.py:139
  77.3 1.6 collective-permute-start.3
  78.9 1.5 collective-permute-start.1
  81.7 5.0 %collective-permute-done.1 = bf16[64,1536]{1,0:T(8,128)(2,1)S(1)} collective-permute-done((bf16[64,1536]{1,0:T(8,128)(2,1)S(1)}, bf16[64,1536]{1,0:T(8,128)(2,1)S(1)}, u32[]{:S(2)}, u32[]{:S(2)}) %collective-permute-start.1) | collective-permute-done | bytes 196640 | tf_op jit(solution)/shard_map/ppermute | solution.py:56
  87.8 1.6 collective-permute-start.30
  90.1 5.0 %collective-permute-done.6 = bf16[2,64,1536]{2,1,0:T(8,128)(2,1)S(1)} collective-permute-done((bf16[2,64,1536]{2,1,0:T(8,128)(2,1)S(1)}, bf16[2,64,1536]{2,1,0:T(8,128)(2,1)S(1)}, u32[]{:S(2)}, u32[]{:S(2)}) %collective-permute-start.6) | collective-permute-done | bytes 393248 | tf_op jit(solution)/shard_map/ppermute | solution.py:56
  96.7 7.0 %fusion.2 = f32[256,1536]{1,0:T(8,128)S(1)} fusion(bf16[256,3072]{1,0:T(8,128)(2,1)} %all-gather.9.cloned.1.call-done, bf16[3072,3072]{1,0:T(8,128)(2,1)} %param.4), kind=kOutput, calls=%fused_computation.3 | convolution fusion | flops 2415919104 | bytes 12582912 | tf_op jit(solution)/shard_map/dot_general | solution.py:139
  103.7 5.3 %fusion.10 = f32[256,1536]{1,0:T(8,128)S(1)} fusion(bf16[256,3072]{1,0:T(8,128)(2,1)S(1)} %copy-done.24, bf16[3072,3072]{1,0:T(8,128)(2,1)} %param.4), kind=kOutput, calls=%fused_computation.11 | convolution fusion | flops 2415919104 | bytes 12582912 | tf_op jit(solution)/shard_map/dot_general | solution.py:139
  109.6 1.5 collective-permute-start.5
  112.5 1.5 collective-permute-start.8
  116.4 1.5 collective-permute-start.29
  123.5 2.6 collective-permute-done.10
  126.1 1.5 collective-permute-start.24
  127.9 5.8 %fusion = f32[256,1536]{1,0:T(8,128)S(1)} fusion(bf16[256,3072]{1,0:T(8,128)(2,1)} %all-gather.11.cloned.1.call-done, bf16[3072,3072]{1,0:T(8,128)(2,1)} %param.4), kind=kOutput, calls=%fused_computation.1 | convolution fusion | flops 2415919104 | bytes 12582912 | tf_op jit(solution)/shard_map/dot_general | solution.py:139
  133.7 5.4 %fusion.8 = f32[256,1536]{1,0:T(8,128)S(1)} fusion(bf16[256,3072]{1,0:T(8,128)(2,1)S(1)} %copy-done.25, bf16[3072,3072]{1,0:T(8,128)(2,1)} %param.4), kind=kOutput, calls=%fused_computation.9 | convolution fusion | flops 2415919104 | bytes 12582912 | tf_op jit(solution)/shard_map/dot_general | solution.py:139
  139.1 1.1 select_bitcast_fusion.1
  141.8 1.1 select_bitcast_fusion.3
  143.1 9.2 %fusion.108 = f32[256,3072]{1,0:T(8,128)S(1)} fusion(bf16[3072,3072]{1,0:T(8,128)(2,1)} %param.4, bf16[256,1536]{1,0:T(8,128)(2,1)S(1)} %bitcast.393, bf16[256,1536]{1,0:T(8,128)(2,1)S(1)} %bitcast.396), kind=kOutput, calls=%fused_computation.247 | convolution fusion | flops 4834983936 | bytes 23592960 | tf_op jit(solution)/shard_map/dot_general | solution.py:165
  152.9 1.5 collective-permute-start.9
  156.1 1.6 collective-permute-start.12
  162.1 1.5 collective-permute-start.25
  167.2 1.5 collective-permute-start.22
  169.7 1.5 collective-permute-start.20
  172.1 1.7 copy.34
  173.9 2.6 copy.35
  176.4 2.6 copy.36
  179.1 2.6 copy.37
  183.3 1.2 select_bitcast_fusion.5
  188.2 1.6 collective-permute-start.23
  189.8 1.2 select_bitcast_fusion.27
  192.5 1.5 collective-permute-start.21
  195.2 3.3 %maximum_bitcast_fusion.a_ref = bf16[3072,1024]{1,0:T(8,128)(2,1)} fusion(bf16[256,3072]{0,1:T(8,128)(2,1)S(1)} %copy-done.2, bf16[256,3072]{0,1:T(8,128)(2,1)S(1)} %copy-done.1, bf16[256,3072]{0,1:T(8,128)(2,1)S(1)} %copy-done, bf16[256,3072]{0,1:T(8,128)(2,1)S(1)} %copy.34), kind=kLoop, calls=%fused_computation | loop fusion | flops 25165824 | bytes 12582912 | tf_op jit(solution)/shard_map/transpose | solution.py:176
  201.6 1.3 pad_maximum_fusion
  203.0 1.1 copy-done.6
  204.1 1.3 bitcast_add_fusion.3
  205.5 1.5 collective-permute-start.36
  206.9 9.0 %fusion.111 = f32[256,3072]{1,0:T(8,128)S(1)} fusion(bf16[256,3072]{1,0:T(8,128)(2,1)S(1)} %pad_maximum_fusion.3.refs_1_, bf16[3072,3072]{1,0:T(8,128)(2,1)} %param.4), kind=kOutput, calls=%fused_computation.250 | convolution fusion | flops 4831838208 | bytes 23592960 | tf_op jit(solution)/shard_map/dot_general | solution.py:165
  216.1 2.4 collective-permute-start.38
  218.6 1.1 select_bitcast_fusion.9
  222.2 1.6 collective-permute-start.19
  223.8 1.3 collective-permute-start.17
  225.1 4.3 %collective-permute-done.37 = bf16[32,3072]{1,0:T(8,128)(2,1)S(1)} collective-permute-done((bf16[32,3072]{1,0:T(8,128)(2,1)S(1)}, bf16[32,3072]{1,0:T(8,128)(2,1)S(1)}, u32[]{:S(2)}, u32[]{:S(2)}) %collective-permute-start.37) | collective-permute-done | bytes 196640 | tf_op jit(solution)/shard_map/ppermute | solution.py:99
  229.5 4.3 %collective-permute-done.19 = bf16[2,64,1536]{2,1,0:T(8,128)(2,1)S(1)} collective-permute-done((bf16[2,64,1536]{2,1,0:T(8,128)(2,1)S(1)}, bf16[2,64,1536]{2,1,0:T(8,128)(2,1)S(1)}, u32[]{:S(2)}, u32[]{:S(2)}) %collective-permute-start.19) | collective-permute-done | bytes 393248 | tf_op jit(solution)/shard_map/ppermute | solution.py:56
  233.9 1.3 collective-permute-done.17
  235.4 9.0 %fusion.112 = f32[256,3072]{1,0:T(8,128)S(1)} fusion(bf16[256,3072]{1,0:T(8,128)(2,1)S(1)} %pad_maximum_fusion.2.refs_2_, bf16[3072,3072]{1,0:T(8,128)(2,1)} %param.4), kind=kOutput, calls=%fused_computation.251 | convolution fusion | flops 4831838208 | bytes 23592960 | tf_op jit(solution)/shard_map/dot_general | solution.py:165
  246.5 3.2 collective-permute-start.41
  251.4 3.6 %collective-permute-start.44 = (bf16[32,3072]{1,0:T(8,128)(2,1)}, bf16[32,3072]{1,0:T(8,128)(2,1)}, u32[]{:S(2)}, u32[]{:S(2)}) collective-permute-start(bf16[32,3072]{1,0:T(8,128)(2,1)} %get-tuple-element.40), channel_id=1, source_target_pairs={{0,24},{4,28},{8,0},{12,4},{16,8},{20,12},{24,16},{28,20},{1,25},{... | collective-permute-start | bytes 589832 | tf_op jit(solution)/shard_map/ppermute | solution.py:99
  255.0 9.0 %fusion.113 = f32[256,3072]{1,0:T(8,128)S(1)} fusion(bf16[256,3072]{1,0:T(8,128)(2,1)S(1)} %pad_maximum_fusion.1.refs_3_, bf16[3072,3072]{1,0:T(8,128)(2,1)} %param.4), kind=kOutput, calls=%fused_computation.252 | convolution fusion | flops 4831838208 | bytes 23592960 | tf_op jit(solution)/shard_map/dot_general | solution.py:165
  265.7 6.9 %collective-permute-done.40 = bf16[32,3072]{1,0:T(8,128)(2,1)} collective-permute-done((bf16[32,3072]{1,0:T(8,128)(2,1)S(1)}, bf16[32,3072]{1,0:T(8,128)(2,1)}, u32[]{:S(2)}, u32[]{:S(2)}) %collective-permute-start.40) | collective-permute-done | bytes 196640 | tf_op jit(solution)/shard_map/ppermute | solution.py:99
  272.6 1.2 fusion.84
  273.8 10.9 %collective-permute-done.43 = bf16[32,3072]{1,0:T(8,128)(2,1)S(1)} collective-permute-done((bf16[32,3072]{1,0:T(8,128)(2,1)S(1)}, bf16[32,3072]{1,0:T(8,128)(2,1)S(1)}, u32[]{:S(2)}, u32[]{:S(2)}) %collective-permute-start.43) | collective-permute-done | bytes 196640 | tf_op jit(solution)/shard_map/ppermute | solution.py:99
  284.7 1.1 fusion.81
  286.2 3.8 %collective-permute-start.47 = (bf16[32,3072]{1,0:T(8,128)(2,1)S(1)}, bf16[32,3072]{1,0:T(8,128)(2,1)S(1)}, u32[]{:S(2)}, u32[]{:S(2)}) collective-permute-start(bf16[32,3072]{1,0:T(8,128)(2,1)S(1)} %get-tuple-element.43), channel_id=1, source_target_pairs={{0,24},{4,28},{8,0},{12,4},{16,8},{20,12},{24,16},{28,20},{1,25},{... | collective-permute-start | bytes 589832 | tf_op jit(solution)/shard_map/ppermute | solution.py:99
  290.0 25.4 %shard_map.58 = f32[3072,3072]{1,0:T(8,128)} custom-call(bf16[3072,1024]{1,0:T(8,128)(2,1)} %maximum_bitcast_fusion.a_ref, bf16[256,3072]{1,0:T(8,128)(2,1)S(1)} %pad_maximum_fusion.4.refs_0_, bf16[256,3072]{1,0:T(8,128)(2,1)S(1)} %pad_maximum_fusion.3.refs_1_, bf16[256,3072]{1,0:T(8,128)(2,1)S(1)} %pad_maximum_fusion.2.refs_2_, bf16[256,3072]{1,0:T(8,128)(2,1)} %copy-done.26), custom_call_target="tpu_custom_call" | custom-call | flops 19327352832 | bytes 50331648 | tf_op jit(solution)/shard_map/pallas_call | solution.py:38
  (231 shorter events, 53.3 us)
Async XLA Ops:
  7.2 30.8 %all-gather.5.cloned.1.call-start = ((), (), s32[]{:S(2)}) async-start(), calls=%async_computation | async-start | bytes 1769472 | tf_op jit(solution)/shard_map/all_gather | solution.py:129
  9.5 55.4 %all-gather.7.cloned.1.call-start = ((), (), s32[]{:S(2)}) async-start(), calls=%async_computation.1 | async-start | bytes 1769472 | tf_op jit(solution)/shard_map/all_gather | solution.py:129
  10.2 86.5 %all-gather.9.cloned.1.call-start = ((), (), s32[]{:S(2)}) async-start(), calls=%async_computation.2 | async-start | bytes 1769472 | tf_op jit(solution)/shard_map/all_gather | solution.py:129
  10.9 116.9 %all-gather.11.cloned.1.call-start = ((), (), s32[]{:S(2)}) async-start(), calls=%async_computation.3 | async-start | bytes 1769472 | tf_op jit(solution)/shard_map/all_gather | solution.py:129
  38.0 8.4 %copy-start.22 = (bf16[256,3072]{1,0:T(8,128)(2,1)S(1)}, bf16[256,3072]{1,0:T(8,128)(2,1)}, u32[]{:S(2)}) copy-start(bf16[256,3072]{1,0:T(8,128)(2,1)} %all-gather.5.cloned.1.call-done) | copy-start | bytes 4718596
  44.9 11.3 %collective-permute-start.2 = (bf16[2,64,1536]{2,1,0:T(8,128)(2,1)S(1)}, bf16[2,64,1536]{2,1,0:T(8,128)(2,1)S(1)}, u32[]{:S(2)}, u32[]{:S(2)}) collective-permute-start(bf16[2,64,1536]{2,1,0:T(8,128)(2,1)S(1)} %fusion.68), channel_id=1, source_target_pairs={{0,2},{1,3},{2,0},{3,1},{4,6},{5,7},{6,4},{7,5},{8,10},{9,11},{10,... | collective-permute-start | bytes 1179656 | tf_op jit(solution)/shard_map/ppermute | solution.py:56
  51.9 11.1 %collective-permute-start = (bf16[2,64,1536]{2,1,0:T(8,128)(2,1)S(1)}, bf16[2,64,1536]{2,1,0:T(8,128)(2,1)S(1)}, u32[]{:S(2)}, u32[]{:S(2)}) collective-permute-start(bf16[2,64,1536]{2,1,0:T(8,128)(2,1)S(1)} %fusion.72), channel_id=1, source_target_pairs={{0,1},{1,0},{2,3},{3,2},{4,5},{5,4},{6,7},{7,6},{8,9},{9,8},{10,11... | collective-permute-start | bytes 1179656 | tf_op jit(solution)/shard_map/ppermute | solution.py:56
  64.8 7.0 %copy-start.23 = (bf16[256,3072]{1,0:T(8,128)(2,1)S(1)}, bf16[256,3072]{1,0:T(8,128)(2,1)}, u32[]{:S(2)}) copy-start(bf16[256,3072]{1,0:T(8,128)(2,1)} %all-gather.7.cloned.1.call-done) | copy-start | bytes 4718596
  77.3 10.2 %collective-permute-start.3 = (bf16[64,1536]{1,0:T(8,128)(2,1)S(1)}, bf16[64,1536]{1,0:T(8,128)(2,1)S(1)}, u32[]{:S(2)}, u32[]{:S(2)}) collective-permute-start(bf16[64,1536]{1,0:T(8,128)(2,1)S(1)} %fusion.89), channel_id=1, source_target_pairs={{0,1},{1,0},{2,3},{3,2},{4,5},{5,4},{6,7},{7,6},{8,9},{9,8},{10,11... | collective-permute-start | bytes 589832 | tf_op jit(solution)/shard_map/ppermute | solution.py:56
  78.9 7.8 %collective-permute-start.1 = (bf16[64,1536]{1,0:T(8,128)(2,1)S(1)}, bf16[64,1536]{1,0:T(8,128)(2,1)S(1)}, u32[]{:S(2)}, u32[]{:S(2)}) collective-permute-start(bf16[64,1536]{1,0:T(8,128)(2,1)S(1)} %fusion.88), channel_id=1, source_target_pairs={{0,2},{1,3},{2,0},{3,1},{4,6},{5,7},{6,4},{7,5},{8,10},{9,11},{10,... | collective-permute-start | bytes 589832 | tf_op jit(solution)/shard_map/ppermute | solution.py:56
  80.4 14.7 %collective-permute-start.6 = (bf16[2,64,1536]{2,1,0:T(8,128)(2,1)S(1)}, bf16[2,64,1536]{2,1,0:T(8,128)(2,1)S(1)}, u32[]{:S(2)}, u32[]{:S(2)}) collective-permute-start(bf16[2,64,1536]{2,1,0:T(8,128)(2,1)S(1)} %fusion.69), channel_id=1, source_target_pairs={{0,2},{1,3},{2,0},{3,1},{4,6},{5,7},{6,4},{7,5},{8,10},{9,11},{10,... | collective-permute-start | bytes 1179656 | tf_op jit(solution)/shard_map/ppermute | solution.py:56
  81.1 14.8 %collective-permute-start.4 = (bf16[2,64,1536]{2,1,0:T(8,128)(2,1)S(1)}, bf16[2,64,1536]{2,1,0:T(8,128)(2,1)S(1)}, u32[]{:S(2)}, u32[]{:S(2)}) collective-permute-start(bf16[2,64,1536]{2,1,0:T(8,128)(2,1)S(1)} %fusion.73), channel_id=1, source_target_pairs={{0,1},{1,0},{2,3},{3,2},{4,5},{5,4},{6,7},{7,6},{8,9},{9,8},{10,11... | collective-permute-start | bytes 1179656 | tf_op jit(solution)/shard_map/ppermute | solution.py:56
  86.9 24.9 %collective-permute-start.28 = (bf16[64,1536]{1,0:T(8,128)(2,1)S(1)}, bf16[64,1536]{1,0:T(8,128)(2,1)S(1)}, u32[]{:S(2)}, u32[]{:S(2)}) collective-permute-start(bf16[64,1536]{1,0:T(8,128)(2,1)S(1)} %get-tuple-element.53), channel_id=1, source_target_pairs={{0,1},{1,0},{2,3},{3,2},{4,5},{5,4},{6,7},{7,6},{8,9},{9,8},{10,11... | collective-permute-start | bytes 589832 | tf_op jit(solution)/shard_map/ppermute | solution.py:56
  87.8 28.0 %collective-permute-start.30 = (bf16[64,1536]{1,0:T(8,128)(2,1)S(1)}, bf16[64,1536]{1,0:T(8,128)(2,1)S(1)}, u32[]{:S(2)}, u32[]{:S(2)}) collective-permute-start(bf16[64,1536]{1,0:T(8,128)(2,1)S(1)} %get-tuple-element.55), channel_id=1, source_target_pairs={{0,2},{1,3},{2,0},{3,1},{4,6},{5,7},{6,4},{7,5},{8,10},{9,11},{10,... | collective-permute-start | bytes 589832 | tf_op jit(solution)/shard_map/ppermute | solution.py:56
  96.7 7.0 %copy-start.24 = (bf16[256,3072]{1,0:T(8,128)(2,1)S(1)}, bf16[256,3072]{1,0:T(8,128)(2,1)}, u32[]{:S(2)}) copy-start(bf16[256,3072]{1,0:T(8,128)(2,1)} %all-gather.9.cloned.1.call-done) | copy-start | bytes 4718596
  109.1 10.7 %collective-permute-start.7 = (bf16[64,1536]{1,0:T(8,128)(2,1)}, bf16[64,1536]{1,0:T(8,128)(2,1)S(1)}, u32[]{:S(2)}, u32[]{:S(2)}) collective-permute-start(bf16[64,1536]{1,0:T(8,128)(2,1)} %fusion.91), channel_id=1, source_target_pairs={{0,1},{1,0},{2,3},{3,2},{4,5},{5,4},{6,7},{7,6},{8,9},{9,8},{10,11... | collective-permute-start | bytes 589832 | tf_op jit(solution)/shard_map/ppermute | solution.py:56
  109.6 11.6 %collective-permute-start.5 = (bf16[64,1536]{1,0:T(8,128)(2,1)}, bf16[64,1536]{1,0:T(8,128)(2,1)S(1)}, u32[]{:S(2)}, u32[]{:S(2)}) collective-permute-start(bf16[64,1536]{1,0:T(8,128)(2,1)} %fusion.90), channel_id=1, source_target_pairs={{0,2},{1,3},{2,0},{3,1},{4,6},{5,7},{6,4},{7,5},{8,10},{9,11},{10,... | collective-permute-start | bytes 589832 | tf_op jit(solution)/shard_map/ppermute | solution.py:56
  111.2 14.9 %collective-permute-start.10 = (bf16[2,64,1536]{2,1,0:T(8,128)(2,1)S(1)}, bf16[2,64,1536]{2,1,0:T(8,128)(2,1)S(1)}, u32[]{:S(2)}, u32[]{:S(2)}) collective-permute-start(bf16[2,64,1536]{2,1,0:T(8,128)(2,1)S(1)} %fusion.70), channel_id=1, source_target_pairs={{0,2},{1,3},{2,0},{3,1},{4,6},{5,7},{6,4},{7,5},{8,10},{9,11},{10,... | collective-permute-start | bytes 1179656 | tf_op jit(solution)/shard_map/ppermute | solution.py:56
  112.5 15.2 %collective-permute-start.8 = (bf16[2,64,1536]{2,1,0:T(8,128)(2,1)S(1)}, bf16[2,64,1536]{2,1,0:T(8,128)(2,1)S(1)}, u32[]{:S(2)}, u32[]{:S(2)}) collective-permute-start(bf16[2,64,1536]{2,1,0:T(8,128)(2,1)S(1)} %fusion.74), channel_id=1, source_target_pairs={{0,1},{1,0},{2,3},{3,2},{4,5},{5,4},{6,7},{7,6},{8,9},{9,8},{10,11... | collective-permute-start | bytes 1179656 | tf_op jit(solution)/shard_map/ppermute | solution.py:56
  116.4 25.3 %collective-permute-start.29 = (bf16[2,64,1536]{2,1,0:T(8,128)(2,1)}, bf16[2,64,1536]{2,1,0:T(8,128)(2,1)}, u32[]{:S(2)}, u32[]{:S(2)}) collective-permute-start(bf16[2,64,1536]{2,1,0:T(8,128)(2,1)} %pad_maximum_fusion.24), channel_id=1, source_target_pairs={{0,2},{1,3},{2,0},{3,1},{4,6},{5,7},{6,4},{7,5},{8,10},{9,11},{10,... | collective-permute-start | bytes 1179656 | tf_op jit(solution)/shard_map/ppermute | solution.py:56
  119.8 19.3 %collective-permute-start.31 = (bf16[2,64,1536]{2,1,0:T(8,128)(2,1)}, bf16[2,64,1536]{2,1,0:T(8,128)(2,1)}, u32[]{:S(2)}, u32[]{:S(2)}) collective-permute-start(bf16[2,64,1536]{2,1,0:T(8,128)(2,1)} %pad_maximum_fusion.25), channel_id=1, source_target_pairs={{0,1},{1,0},{2,3},{3,2},{4,5},{5,4},{6,7},{7,6},{8,9},{9,8},{10,11... | collective-permute-start | bytes 1179656 | tf_op jit(solution)/shard_map/ppermute | solution.py:56
  121.2 34.9 %collective-permute-start.26 = (bf16[64,1536]{1,0:T(8,128)(2,1)}, bf16[64,1536]{1,0:T(8,128)(2,1)}, u32[]{:S(2)}, u32[]{:S(2)}) collective-permute-start(bf16[64,1536]{1,0:T(8,128)(2,1)} %get-tuple-element.59), channel_id=1, source_target_pairs={{0,2},{1,3},{2,0},{3,1},{4,6},{5,7},{6,4},{7,5},{8,10},{9,11},{10,... | collective-permute-start | bytes 589832 | tf_op jit(solution)/shard_map/ppermute | solution.py:56
  126.1 33.6 %collective-permute-start.24 = (bf16[64,1536]{1,0:T(8,128)(2,1)}, bf16[64,1536]{1,0:T(8,128)(2,1)}, u32[]{:S(2)}, u32[]{:S(2)}) collective-permute-start(bf16[64,1536]{1,0:T(8,128)(2,1)} %get-tuple-element.57), channel_id=1, source_target_pairs={{0,1},{1,0},{2,3},{3,2},{4,5},{5,4},{6,7},{7,6},{8,9},{9,8},{10,11... | collective-permute-start | bytes 589832 | tf_op jit(solution)/shard_map/ppermute | solution.py:56
  127.9 5.8 %copy-start.25 = (bf16[256,3072]{1,0:T(8,128)(2,1)S(1)}, bf16[256,3072]{1,0:T(8,128)(2,1)}, u32[]{:S(2)}) copy-start(bf16[256,3072]{1,0:T(8,128)(2,1)} %all-gather.11.cloned.1.call-done) | copy-start | bytes 4718596
  133.6 5.5 %copy-start.18 = (bf16[1,64,1536]{2,1,0:T(8,128)(2,1)S(1)}, bf16[1,64,1536]{2,1,0:T(8,128)(2,1)}, u32[]{:S(2)}) copy-start(bf16[1,64,1536]{2,1,0:T(8,128)(2,1)} %copy-done.17) | copy-start | bytes 589828
  133.7 5.5 %copy-start.20 = (bf16[1,64,1536]{2,1,0:T(8,128)(2,1)S(1)}, bf16[1,64,1536]{2,1,0:T(8,128)(2,1)}, u32[]{:S(2)}) copy-start(bf16[1,64,1536]{2,1,0:T(8,128)(2,1)} %copy-done.19) | copy-start | bytes 589828
  152.3 12.2 %collective-permute-start.11 = (bf16[64,1536]{1,0:T(8,128)(2,1)}, bf16[64,1536]{1,0:T(8,128)(2,1)S(1)}, u32[]{:S(2)}, u32[]{:S(2)}) collective-permute-start(bf16[64,1536]{1,0:T(8,128)(2,1)} %fusion.93), channel_id=1, source_target_pairs={{0,1},{1,0},{2,3},{3,2},{4,5},{5,4},{6,7},{7,6},{8,9},{9,8},{10,11... | collective-permute-start | bytes 589832 | tf_op jit(solution)/shard_map/ppermute | solution.py:56
  152.9 9.2 %collective-permute-start.9 = (bf16[64,1536]{1,0:T(8,128)(2,1)}, bf16[64,1536]{1,0:T(8,128)(2,1)S(1)}, u32[]{:S(2)}, u32[]{:S(2)}) collective-permute-start(bf16[64,1536]{1,0:T(8,128)(2,1)} %fusion.92), channel_id=1, source_target_pairs={{0,2},{1,3},{2,0},{3,1},{4,6},{5,7},{6,4},{7,5},{8,10},{9,11},{10,... | collective-permute-start | bytes 589832 | tf_op jit(solution)/shard_map/ppermute | solution.py:56
  154.4 12.8 %collective-permute-start.14 = (bf16[2,64,1536]{2,1,0:T(8,128)(2,1)S(1)}, bf16[2,64,1536]{2,1,0:T(8,128)(2,1)S(1)}, u32[]{:S(2)}, u32[]{:S(2)}) collective-permute-start(bf16[2,64,1536]{2,1,0:T(8,128)(2,1)S(1)} %fusion.71), channel_id=1, source_target_pairs={{0,2},{1,3},{2,0},{3,1},{4,6},{5,7},{6,4},{7,5},{8,10},{9,11},{10,... | collective-permute-start | bytes 1179656 | tf_op jit(solution)/shard_map/ppermute | solution.py:56
  156.1 7.5 %copy-start.33 = (bf16[2,1,32,1536]{3,2,1,0:T(8,128)(2,1)S(1)}, bf16[2,1,32,1536]{3,2,1,0:T(8,128)(2,1)}, u32[]{:S(2)}) copy-start(bf16[2,1,32,1536]{3,2,1,0:T(8,128)(2,1)} %get-tuple-element.50) | copy-start | bytes 589828
  156.1 13.6 %collective-permute-start.12 = (bf16[2,64,1536]{2,1,0:T(8,128)(2,1)S(1)}, bf16[2,64,1536]{2,1,0:T(8,128)(2,1)S(1)}, u32[]{:S(2)}, u32[]{:S(2)}) collective-permute-start(bf16[2,64,1536]{2,1,0:T(8,128)(2,1)S(1)} %fusion.75), channel_id=1, source_target_pairs={{0,1},{1,0},{2,3},{3,2},{4,5},{5,4},{6,7},{7,6},{8,9},{9,8},{10,11... | collective-permute-start | bytes 1179656 | tf_op jit(solution)/shard_map/ppermute | solution.py:56
  158.8 6.7 %copy-start.15 = (bf16[1,64,1536]{2,1,0:T(8,128)(2,1)}, bf16[1,64,1536]{2,1,0:T(8,128)(2,1)S(1)}, u32[]{:S(2)}) copy-start(bf16[1,64,1536]{2,1,0:T(8,128)(2,1)S(1)} %get-tuple-element.95) | copy-start | bytes 589828
  158.8 6.7 %copy-start.16 = (bf16[1,64,1536]{2,1,0:T(8,128)(2,1)}, bf16[1,64,1536]{2,1,0:T(8,128)(2,1)S(1)}, u32[]{:S(2)}) copy-start(bf16[1,64,1536]{2,1,0:T(8,128)(2,1)S(1)} %get-tuple-element.96) | copy-start | bytes 589828
  159.7 4.8 %copy-start.32 = (bf16[2,1,32,1536]{3,2,1,0:T(8,128)(2,1)S(1)}, bf16[2,1,32,1536]{3,2,1,0:T(8,128)(2,1)}, u32[]{:S(2)}) copy-start(bf16[2,1,32,1536]{3,2,1,0:T(8,128)(2,1)} %get-tuple-element.49) | copy-start | bytes 589828
  159.7 23.0 %collective-permute-start.27 = (bf16[2,64,1536]{2,1,0:T(8,128)(2,1)}, bf16[2,64,1536]{2,1,0:T(8,128)(2,1)}, u32[]{:S(2)}, u32[]{:S(2)}) collective-permute-start(bf16[2,64,1536]{2,1,0:T(8,128)(2,1)} %pad_maximum_fusion.23), channel_id=1, source_target_pairs={{0,1},{1,0},{2,3},{3,2},{4,5},{5,4},{6,7},{7,6},{8,9},{9,8},{10,11... | collective-permute-start | bytes 1179656 | tf_op jit(solution)/shard_map/ppermute | solution.py:56
  162.1 30.5 %collective-permute-start.25 = (bf16[2,64,1536]{2,1,0:T(8,128)(2,1)}, bf16[2,64,1536]{2,1,0:T(8,128)(2,1)}, u32[]{:S(2)}, u32[]{:S(2)}) collective-permute-start(bf16[2,64,1536]{2,1,0:T(8,128)(2,1)} %pad_maximum_fusion.22), channel_id=1, source_target_pairs={{0,2},{1,3},{2,0},{3,1},{4,6},{5,7},{6,4},{7,5},{8,10},{9,11},{10,... | collective-permute-start | bytes 1179656 | tf_op jit(solution)/shard_map/ppermute | solution.py:56
  164.5 38.5 %collective-permute-start.32 = (bf16[4,32,3072]{2,1,0:T(8,128)(2,1)}, bf16[4,32,3072]{2,1,0:T(8,128)(2,1)}, u32[]{:S(2)}, u32[]{:S(2)}) collective-permute-start(bf16[4,32,3072]{2,1,0:T(8,128)(2,1)} %fusion.16), channel_id=1, source_target_pairs={{0,4},{4,0},{8,12},{12,8},{16,20},{20,16},{24,28},{28,24},{1,5},{5... | collective-permute-start | bytes 2359304 | tf_op jit(solution)/shard_map/ppermute | solution.py:88
  167.2 18.4 %collective-permute-start.22 = (bf16[64,1536]{1,0:T(8,128)(2,1)}, bf16[64,1536]{1,0:T(8,128)(2,1)}, u32[]{:S(2)}, u32[]{:S(2)}) collective-permute-start(bf16[64,1536]{1,0:T(8,128)(2,1)} %get-tuple-element.63), channel_id=1, source_target_pairs={{0,2},{1,3},{2,0},{3,1},{4,6},{5,7},{6,4},{7,5},{8,10},{9,11},{10,... | collective-permute-start | bytes 589832 | tf_op jit(solution)/shard_map/ppermute | solution.py:56
  169.7 18.5 %collective-permute-start.20 = (bf16[64,1536]{1,0:T(8,128)(2,1)}, bf16[64,1536]{1,0:T(8,128)(2,1)}, u32[]{:S(2)}, u32[]{:S(2)}) collective-permute-start(bf16[64,1536]{1,0:T(8,128)(2,1)} %get-tuple-element.61), channel_id=1, source_target_pairs={{0,1},{1,0},{2,3},{3,2},{4,5},{5,4},{6,7},{7,6},{8,9},{9,8},{10,11... | collective-permute-start | bytes 589832 | tf_op jit(solution)/shard_map/ppermute | solution.py:56
  182.7 16.0 %collective-permute-start.15 = (bf16[64,1536]{1,0:T(8,128)(2,1)S(1)}, bf16[64,1536]{1,0:T(8,128)(2,1)S(1)}, u32[]{:S(2)}, u32[]{:S(2)}) collective-permute-start(bf16[64,1536]{1,0:T(8,128)(2,1)S(1)} %fusion.95), channel_id=1, source_target_pairs={{0,1},{1,0},{2,3},{3,2},{4,5},{5,4},{6,7},{7,6},{8,9},{9,8},{10,11... | collective-permute-start | bytes 589832 | tf_op jit(solution)/shard_map/ppermute | solution.py:56
  185.6 15.1 %collective-permute-start.13 = (bf16[64,1536]{1,0:T(8,128)(2,1)S(1)}, bf16[64,1536]{1,0:T(8,128)(2,1)S(1)}, u32[]{:S(2)}, u32[]{:S(2)}) collective-permute-start(bf16[64,1536]{1,0:T(8,128)(2,1)S(1)} %fusion.94), channel_id=1, source_target_pairs={{0,2},{1,3},{2,0},{3,1},{4,6},{5,7},{6,4},{7,5},{8,10},{9,11},{10,... | collective-permute-start | bytes 589832 | tf_op jit(solution)/shard_map/ppermute | solution.py:56
  188.2 27.9 %collective-permute-start.23 = (bf16[2,64,1536]{2,1,0:T(8,128)(2,1)}, bf16[2,64,1536]{2,1,0:T(8,128)(2,1)}, u32[]{:S(2)}, u32[]{:S(2)}) collective-permute-start(bf16[2,64,1536]{2,1,0:T(8,128)(2,1)} %pad_maximum_fusion.21), channel_id=1, source_target_pairs={{0,1},{1,0},{2,3},{3,2},{4,5},{5,4},{6,7},{7,6},{8,9},{9,8},{10,11... | collective-permute-start | bytes 1179656 | tf_op jit(solution)/shard_map/ppermute | solution.py:56
  189.8 5.3 %copy-start.2 = (bf16[256,3072]{0,1:T(8,128)(2,1)S(1)}, bf16[256,3072]{0,1:T(8,128)(2,1)}, u32[]{:S(2)}) copy-start(bf16[256,3072]{0,1:T(8,128)(2,1)} %copy.37) | copy-start | bytes 4718596
  192.5 27.3 %collective-permute-start.21 = (bf16[2,64,1536]{2,1,0:T(8,128)(2,1)}, bf16[2,64,1536]{2,1,0:T(8,128)(2,1)}, u32[]{:S(2)}, u32[]{:S(2)}) collective-permute-start(bf16[2,64,1536]{2,1,0:T(8,128)(2,1)} %pad_maximum_fusion.20), channel_id=1, source_target_pairs={{0,2},{1,3},{2,0},{3,1},{4,6},{5,7},{6,4},{7,5},{8,10},{9,11},{10,... | collective-permute-start | bytes 1179656 | tf_op jit(solution)/shard_map/ppermute | solution.py:56
  199.9 22.1 %collective-permute-start.18 = (bf16[64,1536]{1,0:T(8,128)(2,1)S(1)}, bf16[64,1536]{1,0:T(8,128)(2,1)S(1)}, u32[]{:S(2)}, u32[]{:S(2)}) collective-permute-start(bf16[64,1536]{1,0:T(8,128)(2,1)S(1)} %get-tuple-element.67), channel_id=1, source_target_pairs={{0,2},{1,3},{2,0},{3,1},{4,6},{5,7},{6,4},{7,5},{8,10},{9,11},{10,... | collective-permute-start | bytes 589832 | tf_op jit(solution)/shard_map/ppermute | solution.py:56
  201.0 21.2 %collective-permute-start.16 = (bf16[64,1536]{1,0:T(8,128)(2,1)S(1)}, bf16[64,1536]{1,0:T(8,128)(2,1)S(1)}, u32[]{:S(2)}, u32[]{:S(2)}) collective-permute-start(bf16[64,1536]{1,0:T(8,128)(2,1)S(1)} %get-tuple-element.65), channel_id=1, source_target_pairs={{0,1},{1,0},{2,3},{3,2},{4,5},{5,4},{6,7},{7,6},{8,9},{9,8},{10,11... | collective-permute-start | bytes 589832 | tf_op jit(solution)/shard_map/ppermute | solution.py:56
  205.5 18.4 %collective-permute-start.36 = (bf16[32,3072]{1,0:T(8,128)(2,1)S(1)}, bf16[32,3072]{1,0:T(8,128)(2,1)S(1)}, u32[]{:S(2)}, u32[]{:S(2)}) collective-permute-start(bf16[32,3072]{1,0:T(8,128)(2,1)S(1)} %get-tuple-element.33), channel_id=1, source_target_pairs={{0,8},{4,12},{8,16},{12,20},{16,24},{20,28},{24,0},{28,4},{1,9},{5... | collective-permute-start | bytes 589832 | tf_op jit(solution)/shard_map/ppermute | solution.py:99
  216.1 9.0 %collective-permute-start.38 = (bf16[32,3072]{1,0:T(8,128)(2,1)S(1)}, bf16[32,3072]{1,0:T(8,128)(2,1)S(1)}, u32[]{:S(2)}, u32[]{:S(2)}) collective-permute-start(bf16[32,3072]{1,0:T(8,128)(2,1)S(1)} %get-tuple-element.34), channel_id=1, source_target_pairs={{0,24},{4,28},{8,0},{12,4},{16,8},{20,12},{24,16},{28,20},{1,25},{... | collective-permute-start | bytes 589832 | tf_op jit(solution)/shard_map/ppermute | solution.py:99
  219.8 9.6 %collective-permute-start.37 = (bf16[32,3072]{1,0:T(8,128)(2,1)S(1)}, bf16[32,3072]{1,0:T(8,128)(2,1)S(1)}, u32[]{:S(2)}, u32[]{:S(2)}) collective-permute-start(bf16[32,3072]{1,0:T(8,128)(2,1)S(1)} %get-tuple-element.35), channel_id=1, source_target_pairs={{0,16},{4,20},{8,24},{12,28},{16,0},{20,4},{24,8},{28,12},{1,17},{... | collective-permute-start | bytes 589832 | tf_op jit(solution)/shard_map/ppermute | solution.py:99
  222.0 13.2 %collective-permute-start.33 = (bf16[4,32,3072]{2,1,0:T(8,128)(2,1)S(1)}, bf16[4,32,3072]{2,1,0:T(8,128)(2,1)S(1)}, u32[]{:S(2)}, u32[]{:S(2)}) collective-permute-start(bf16[4,32,3072]{2,1,0:T(8,128)(2,1)S(1)} %fusion.17), channel_id=1, source_target_pairs={{0,4},{4,0},{8,12},{12,8},{16,20},{20,16},{24,28},{28,24},{1,5},{5... | collective-permute-start | bytes 2359304 | tf_op jit(solution)/shard_map/ppermute | solution.py:88
  222.2 11.6 %collective-permute-start.19 = (bf16[2,64,1536]{2,1,0:T(8,128)(2,1)S(1)}, bf16[2,64,1536]{2,1,0:T(8,128)(2,1)S(1)}, u32[]{:S(2)}, u32[]{:S(2)}) collective-permute-start(bf16[2,64,1536]{2,1,0:T(8,128)(2,1)S(1)} %pad_maximum_fusion.19), channel_id=1, source_target_pairs={{0,1},{1,0},{2,3},{3,2},{4,5},{5,4},{6,7},{7,6},{8,9},{9,8},{10,11... | collective-permute-start | bytes 1179656 | tf_op jit(solution)/shard_map/ppermute | solution.py:56
  223.8 11.3 %collective-permute-start.17 = (bf16[2,64,1536]{2,1,0:T(8,128)(2,1)S(1)}, bf16[2,64,1536]{2,1,0:T(8,128)(2,1)S(1)}, u32[]{:S(2)}, u32[]{:S(2)}) collective-permute-start(bf16[2,64,1536]{2,1,0:T(8,128)(2,1)S(1)} %pad_maximum_fusion.18), channel_id=1, source_target_pairs={{0,2},{1,3},{2,0},{3,1},{4,6},{5,7},{6,4},{7,5},{8,10},{9,11},{10,... | collective-permute-start | bytes 1179656 | tf_op jit(solution)/shard_map/ppermute | solution.py:56
  244.6 5.5 %collective-permute-start.34 = (bf16[4,32,3072]{2,1,0:T(8,128)(2,1)S(1)}, bf16[4,32,3072]{2,1,0:T(8,128)(2,1)S(1)}, u32[]{:S(2)}, u32[]{:S(2)}) collective-permute-start(bf16[4,32,3072]{2,1,0:T(8,128)(2,1)S(1)} %fusion.18), channel_id=1, source_target_pairs={{0,4},{4,0},{8,12},{12,8},{16,20},{20,16},{24,28},{28,24},{1,5},{5... | collective-permute-start | bytes 2359304 | tf_op jit(solution)/shard_map/ppermute | solution.py:88
  244.9 10.0 %copy-start.26 = (bf16[256,3072]{1,0:T(8,128)(2,1)}, bf16[256,3072]{1,0:T(8,128)(2,1)S(1)}, u32[]{:S(2)}) copy-start(bf16[256,3072]{1,0:T(8,128)(2,1)S(1)} %pad_maximum_fusion.1.refs_3_) | copy-start | bytes 4718596
  245.9 18.2 %collective-permute-start.39 = (bf16[32,3072]{1,0:T(8,128)(2,1)}, bf16[32,3072]{1,0:T(8,128)(2,1)}, u32[]{:S(2)}, u32[]{:S(2)}) collective-permute-start(bf16[32,3072]{1,0:T(8,128)(2,1)} %get-tuple-element.36), channel_id=1, source_target_pairs={{0,8},{4,12},{8,16},{12,20},{16,24},{20,28},{24,0},{28,4},{1,9},{5... | collective-permute-start | bytes 589832 | tf_op jit(solution)/shard_map/ppermute | solution.py:99
  246.5 19.2 %collective-permute-start.41 = (bf16[32,3072]{1,0:T(8,128)(2,1)}, bf16[32,3072]{1,0:T(8,128)(2,1)}, u32[]{:S(2)}, u32[]{:S(2)}) collective-permute-start(bf16[32,3072]{1,0:T(8,128)(2,1)} %get-tuple-element.37), channel_id=1, source_target_pairs={{0,24},{4,28},{8,0},{12,4},{16,8},{20,12},{24,16},{28,20},{1,25},{... | collective-permute-start | bytes 589832 | tf_op jit(solution)/shard_map/ppermute | solution.py:99
  249.7 22.9 %collective-permute-start.40 = (bf16[32,3072]{1,0:T(8,128)(2,1)S(1)}, bf16[32,3072]{1,0:T(8,128)(2,1)}, u32[]{:S(2)}, u32[]{:S(2)}) collective-permute-start(bf16[32,3072]{1,0:T(8,128)(2,1)S(1)} %get-tuple-element.38), channel_id=1, source_target_pairs={{0,16},{4,20},{8,24},{12,28},{16,0},{20,4},{24,8},{28,12},{1,17},{... | collective-permute-start | bytes 589832 | tf_op jit(solution)/shard_map/ppermute | solution.py:99
  251.1 22.7 %collective-permute-start.42 = (bf16[32,3072]{1,0:T(8,128)(2,1)}, bf16[32,3072]{1,0:T(8,128)(2,1)}, u32[]{:S(2)}, u32[]{:S(2)}) collective-permute-start(bf16[32,3072]{1,0:T(8,128)(2,1)} %get-tuple-element.39), channel_id=1, source_target_pairs={{0,8},{4,12},{8,16},{12,20},{16,24},{20,28},{24,0},{28,4},{1,9},{5... | collective-permute-start | bytes 589832 | tf_op jit(solution)/shard_map/ppermute | solution.py:99
  251.4 22.5 %collective-permute-start.44 = (bf16[32,3072]{1,0:T(8,128)(2,1)}, bf16[32,3072]{1,0:T(8,128)(2,1)}, u32[]{:S(2)}, u32[]{:S(2)}) collective-permute-start(bf16[32,3072]{1,0:T(8,128)(2,1)} %get-tuple-element.40), channel_id=1, source_target_pairs={{0,24},{4,28},{8,0},{12,4},{16,8},{20,12},{24,16},{28,20},{1,25},{... | collective-permute-start | bytes 589832 | tf_op jit(solution)/shard_map/ppermute | solution.py:99
  264.9 19.8 %collective-permute-start.43 = (bf16[32,3072]{1,0:T(8,128)(2,1)S(1)}, bf16[32,3072]{1,0:T(8,128)(2,1)S(1)}, u32[]{:S(2)}, u32[]{:S(2)}) collective-permute-start(bf16[32,3072]{1,0:T(8,128)(2,1)S(1)} %copy-done.34), channel_id=1, source_target_pairs={{0,16},{4,20},{8,24},{12,28},{16,0},{20,4},{24,8},{28,12},{1,17},{... | collective-permute-start | bytes 589832 | tf_op jit(solution)/shard_map/ppermute | solution.py:99
  265.7 20.1 %collective-permute-start.35 = (bf16[4,32,3072]{2,1,0:T(8,128)(2,1)S(1)}, bf16[4,32,3072]{2,1,0:T(8,128)(2,1)S(1)}, u32[]{:S(2)}, u32[]{:S(2)}) collective-permute-start(bf16[4,32,3072]{2,1,0:T(8,128)(2,1)S(1)} %fusion.19), channel_id=1, source_target_pairs={{0,4},{4,0},{8,12},{12,8},{16,20},{20,16},{24,28},{28,24},{1,5},{5... | collective-permute-start | bytes 2359304 | tf_op jit(solution)/shard_map/ppermute | solution.py:88
  286.1 29.3 %collective-permute-start.45 = (bf16[32,3072]{1,0:T(8,128)(2,1)S(1)}, bf16[32,3072]{1,0:T(8,128)(2,1)S(1)}, u32[]{:S(2)}, u32[]{:S(2)}) collective-permute-start(bf16[32,3072]{1,0:T(8,128)(2,1)S(1)} %get-tuple-element.42), channel_id=1, source_target_pairs={{0,8},{4,12},{8,16},{12,20},{16,24},{20,28},{24,0},{28,4},{1,9},{5... | collective-permute-start | bytes 589832 | tf_op jit(solution)/shard_map/ppermute | solution.py:99
  286.2 29.2 %collective-permute-start.47 = (bf16[32,3072]{1,0:T(8,128)(2,1)S(1)}, bf16[32,3072]{1,0:T(8,128)(2,1)S(1)}, u32[]{:S(2)}, u32[]{:S(2)}) collective-permute-start(bf16[32,3072]{1,0:T(8,128)(2,1)S(1)} %get-tuple-element.43), channel_id=1, source_target_pairs={{0,24},{4,28},{8,0},{12,4},{16,8},{20,12},{24,16},{28,20},{1,25},{... | collective-permute-start | bytes 589832 | tf_op jit(solution)/shard_map/ppermute | solution.py:99
  290.0 25.4 %collective-permute-start.46 = (bf16[32,3072]{1,0:T(8,128)(2,1)S(1)}, bf16[32,3072]{1,0:T(8,128)(2,1)S(1)}, u32[]{:S(2)}, u32[]{:S(2)}) collective-permute-start(bf16[32,3072]{1,0:T(8,128)(2,1)S(1)} %get-tuple-element.44), channel_id=1, source_target_pairs={{0,16},{4,20},{8,24},{12,28},{16,0},{20,4},{24,8},{28,12},{1,17},{... | collective-permute-start | bytes 589832 | tf_op jit(solution)/shard_map/ppermute | solution.py:99
  (25 other events, 48.0 us)
Sparse Core Ops, SparseCore 0:
  10.2 27.7 all-gather.4
  40.2 24.5 all-gather.6
  66.5 24.5 all-gather.8
  93.2 24.5 all-gather.10

commit v3 on v2

--- a/solution.py
+++ b/solution.py
@@ -7,7 +7,7 @@
 from jax.experimental.pallas import tpu as pltpu
 from jax.sharding import PartitionSpec as P
 
-PARTS = 4
+PARTS = 2
 
 
 def gelu_exact(value):
@@ -19,37 +19,37 @@
     return cumulative + value * jnp.exp(-0.5 * value * value) / math.sqrt(2.0 * math.pi)
 
 
-def dot_parts_kernel(a_ref, *refs):
-    parts, out_ref, held = refs[:-2], refs[-2], refs[-1]
-    rows = parts[0].shape[0]
-
-    @pl.when(pl.program_id(0) == 0)
-    def _():
-        for p, part in enumerate(parts):
-            held[p * rows : (p + 1) * rows] = part[...]
-
-    out_ref[...] = jnp.dot(a_ref[...], held[...], preferred_element_type=jnp.float32)
+def dot_parts_kernel(*refs):
+    parts, out_ref = refs[:-1], refs[-1]
+    half = len(parts) // 2
+    total = None
+    for a_ref, b_ref in zip(parts[:half], parts[half:]):
+        term = lax.dot_general(
+            a_ref[...], b_ref[...], (((0,), (0,)), ((), ())), preferred_element_type=jnp.float32
+        )
+        total = term if total is None else total + term
+    out_ref[...] = total
 
 
-def dot_parts(a, parts):
-    m, depth = a.shape
-    rows, n = parts[0].shape
+def dot_parts(a, b):
+    rows, m = a[0].shape
+    n = b[0].shape[1]
     block = 256
+    depth = rows * len(a)
     return pl.pallas_call(
         dot_parts_kernel,
         grid=(m // block,),
-        in_specs=[pl.BlockSpec((block, depth), lambda i: (i, 0))]
-        + [pl.BlockSpec((rows, n), lambda i: (0, 0)) for _ in parts],
+        in_specs=[pl.BlockSpec((rows, block), lambda i: (0, i)) for _ in a]
+        + [pl.BlockSpec((rows, n), lambda i: (0, 0)) for _ in b],
         out_specs=pl.BlockSpec((block, n), lambda i: (i, 0)),
         out_shape=jax.ShapeDtypeStruct((m, n), jnp.float32),
-        scratch_shapes=[pltpu.VMEM((depth, n), jnp.bfloat16)],
         compiler_params=pltpu.CompilerParams(vmem_limit_bytes=48 * 1024 * 1024),
         cost_estimate=pl.CostEstimate(
             flops=2 * depth * m * n,
             bytes_accessed=2 * depth * (m + n) + 4 * m * n,
             transcendentals=0,
         ),
-    )(a, *parts)
+    )(*a, *b)
 
 
 def swap(value, bit):
@@ -101,14 +101,18 @@
     return total.astype(jnp.bfloat16)
 
 
-def gather_square(value, x_first):
+def behind(value, after):
+    return lax.optimization_barrier((value, *after))[0]
+
+
+def gather_square(value, x_first, after):
     me = lax.axis_index("col")
     x, y = me % 2, me // 2
     if x_first:
-        pair = ordered(value, swap(value, 1), x, 0)
+        pair = behind(ordered(value, swap(value, 1), x, 0), after)
         both = ordered(pair, swap(pair, 2), y, 0)
     else:
-        pair = ordered(value, swap(value, 2), y, 0)
+        pair = behind(ordered(value, swap(value, 2), y, 0), after)
         both = ordered(pair, swap(pair, 1), x, 1)
     return both.reshape((4,) + value.shape)
 
@@ -129,7 +133,7 @@
             lax.all_gather(tokens[p * sub : (p + 1) * sub], "row", axis=0, tiled=True)
             for p in range(PARTS)
         ]
-        hiddens, grads, outs = [], [], []
+        hiddens, grads, outs, sent = [], [], [], []
         for p in range(PARTS):
             rows, firsts = gathered[p], []
             if square and p:
@@ -154,14 +158,12 @@
                 hs.append(gelu_exact(pre).astype(jnp.bfloat16))
                 grad_pre = (cot.astype(jnp.float32) * gelu_slope(pre)).astype(jnp.bfloat16)
                 if square:
-                    part = gather_square(grad_pre, h == 0).reshape(-1, wide)
+                    part = gather_square(grad_pre, h == 0, sent).reshape(-1, wide)
                 else:
                     part = lax.all_gather(grad_pre, "col", axis=0, tiled=True)
                 gs.append(part)
             hiddens.append(jnp.concatenate(hs, 1).reshape(blocks, sub, hidden_n))
             grad = jnp.concatenate(gs, 1)
-            if p:
-                grad, _ = lax.optimization_barrier((grad, pairs))
             back = lax.dot_general(
                 grad, weight, (((1,), (1,)), ((), ())), preferred_element_type=jnp.float32
             )
@@ -169,12 +171,11 @@
             pairs = pair_sum(back.reshape(row_n, sub, features), row_n)
             if p == PARTS - 1:
                 pairs, *grads = lax.optimization_barrier((pairs, *grads))
+            sent = [pairs]
             outs.append(scatter_z(pairs, row_n))
         hidden = jnp.stack(hiddens, 1).reshape(owned, hidden_n)
         grad_tokens = jnp.concatenate(outs, 0)
-        *gathered, _ = lax.optimization_barrier((*gathered, held[0]))
-        turned = jnp.concatenate(gathered, 0).T
-        grad_weight = dot_parts(turned, grads)
+        grad_weight = dot_parts(gathered, grads)
         return (hidden, grad_weight, grad_tokens)
 
     return shards

time: 324 us -> 307 us (0.948)
  waiting for transfers between devices: 79.6 us -> 130 us
  starting transfers between devices: 52.5 us -> 25.7 us
  matrix products: 84.5 us -> 67.4 us
  other arithmetic: 38.8 us -> 24.4 us
  local copies, waits for them, and re-layouts: 27.2 us -> 17.9 us
    ppermute x32 -> x16, waiting for transfers between devices: 28.5 us -> 81.8 us  [swap(): return lax.ppermute(value, 'col', [(c, c ^ bit) for c in range(4)])]
    ppermute x32 -> x16, starting transfers between devices: 35.6 us -> 17.7 us  [swap(): return lax.ppermute(value, 'col', [(c, c ^ bit) for c in range(4)])]
    ppermute x12 -> x6, waiting for transfers between devices: 22.1 us -> 6.58 us  [scatter_z(): got = lax.ppermute(block, 'row', [(r, (r + 2 * k) % n) for r in range(n)])]
    all_gather x4 -> x2, waiting for transfers between devices: 27.1 us -> 41.2 us  [shards(): lax.all_gather(tokens[p * sub:(p + 1) * sub], 'row', axis=0, tiled=True)]
    dot_general x8 -> x4, matrix products: 48.2 us -> 35 us  [shards(): partial = jnp.dot(rows, weight[:, cols], preferred_element_type=jnp.float32)]
    another operation x32 -> x16, other arithmetic: 18.6 us -> 6.24 us  [ordered(): return jnp.stack([first, second], axis)]
    optimization_barrier x4 -> x0, local copies, waits for them, and re-layouts: 9.48 us -> none  [shards(): *gathered, _ = lax.optimization_barrier((*gathered, held[0]))]
    ppermute x12 -> x6, starting transfers between devices: 16.6 us -> 7.71 us  [scatter_z(): got = lax.ppermute(block, 'row', [(r, (r + 2 * k) % n) for r in range(n)])]
  transfers between devices with their start and end apart: 52 -> 26, of which waited for: 13 -> 11; matrix products, arithmetic and copies ran while one was open for 41% -> 27% of each run, Pallas kernels for 8% -> 9%
where the time goes in v3:
time: 307 us
  waiting for transfers between devices  130 us (42%)
  matrix products  67.4 us (22%)
  Pallas kernels  27 us (9%)
  starting transfers between devices  25.7 us (8%)
  other arithmetic  24.4 us (8%)
  local copies, waits for them, and re-layouts  17.9 us (6%)
  between operations  14.6 us (5%)
    ppermute x16, waiting for transfers between devices, swap(): return lax.ppermute(value, 'col', [(c, c ^ bit) for c in range(4)])  81.8 us
    all_gather x2, waiting for transfers between devices, shards(): lax.all_gather(tokens[p * sub:(p + 1) * sub], 'row', axis=0, tiled=True)  41.2 us
    dot_general x4, matrix products, shards(): partial = jnp.dot(rows, weight[:, cols], preferred_element_type=jnp.float32)  35 us
    dot_general x2, matrix products, shards(): lax.dot_general(grad, weight, (((1,), (1,)), ((), ())), preferred_element...  32.5 us
    pallas_call x1, Pallas kernels, dot_parts(): pl.pallas_call(dot_parts_kernel, grid=(m // block,), in_specs=[pl.BlockSp...  27 us
    ppermute x16, starting transfers between devices, swap(): return lax.ppermute(value, 'col', [(c, c ^ bit) for c in range(4)])  17.7 us
    ppermute x6, starting transfers between devices, scatter_z(): got = lax.ppermute(block, 'row', [(r, (r + 2 * k) % n) for r in range(n)])  7.71 us
    ppermute x6, waiting for transfers between devices, scatter_z(): got = lax.ppermute(block, 'row', [(r, (r + 2 * k) % n) for r in range(n)])  6.58 us
  transfers between devices with their start and end apart: 26, of which 11 were waited for; matrix products, arithmetic and copies ran while one was open for 27% of the time, Pallas kernels for 9%

profile of v3, /device:TPU:0, one launch (start us, length us, event | category | flops | bytes accessed | tf_op | source)
XLA Modules:
  0.0 307.2 jit_solution(6374751591065775541)
XLA Ops:
  7.2 2.1 fusion.57
  9.3 0.7 all-gather.5.cloned.1.call-update
  10.1 41.2 %all-gather.3.cloned.1.call-done.refs_0_ = bf16[512,3072]{1,0:T(8,128)(2,1)} async-done(((bf16[64,3072]{1,0:T(8,128)(2,1)}), bf16[512,3072]{1,0:T(8,128)(2,1)}) %all-gather.3.cloned.1.call-update) | async-done | bytes 3145744 | tf_op jit(solution)/shard_map/all_gather | solution.py:133
  51.2 9.8 %fusion.2 = f32[512,1536]{1,0:T(8,128)S(1)} fusion(bf16[512,3072]{1,0:T(8,128)(2,1)} %all-gather.3.cloned.1.call-done.refs_0_, bf16[3072,3072]{1,0:T(8,128)(2,1)} %param.4), kind=kOutput, calls=%fused_computation.2 | convolution fusion | flops 4831838208 | bytes 15728640 | tf_op jit(solution)/shard_map/dot_general | solution.py:143
  61.0 1.1 fusion.34
  62.1 0.8 copy-done.16
  62.9 1.5 collective-permute-start.2
  64.4 7.6 %fusion.6 = f32[512,1536]{1,0:T(8,128)S(1)} fusion(bf16[512,3072]{1,0:T(8,128)(2,1)S(1)} %copy-done, bf16[3072,3072]{1,0:T(8,128)(2,1)} %param.4), kind=kOutput, calls=%fused_computation.6 | convolution fusion | flops 4831838208 | bytes 15728640 | tf_op jit(solution)/shard_map/dot_general | solution.py:143
  72.0 1.7 copy-done.14
  73.7 1.0 fusion.36
  74.7 1.5 collective-permute-start
  76.2 1.0 fusion.56
  77.2 5.7 %collective-permute-done.2 = bf16[2,128,1536]{2,1,0:T(8,128)(2,1)} collective-permute-done((bf16[2,128,1536]{2,1,0:T(8,128)(2,1)}, bf16[2,128,1536]{2,1,0:T(8,128)(2,1)}, u32[]{:S(2)}, u32[]{:S(2)}) %collective-permute-start.2) | collective-permute-done | bytes 786464 | tf_op jit(solution)/shard_map/ppermute | solution.py:56
  82.9 1.9 bitcast_add_fusion.4
  84.8 0.9 fusion.45
  86.1 8.3 %collective-permute-done = bf16[2,128,1536]{2,1,0:T(8,128)(2,1)} collective-permute-done((bf16[2,128,1536]{2,1,0:T(8,128)(2,1)}, bf16[2,128,1536]{2,1,0:T(8,128)(2,1)}, u32[]{:S(2)}, u32[]{:S(2)}) %collective-permute-start) | collective-permute-done | bytes 786464 | tf_op jit(solution)/shard_map/ppermute | solution.py:56
  94.4 1.3 bitcast_add_fusion.5
  95.8 1.1 copy-done.7
  96.9 0.8 fusion.44
  97.7 9.7 %fusion = f32[512,1536]{1,0:T(8,128)S(1)} fusion(bf16[512,3072]{1,0:T(8,128)(2,1)} %all-gather.5.cloned.1.call-done.refs_1_, bf16[3072,3072]{1,0:T(8,128)(2,1)} %param.4), kind=kOutput, calls=%fused_computation | convolution fusion | flops 4831838208 | bytes 15728640 | tf_op jit(solution)/shard_map/dot_general | solution.py:143
  107.5 7.9 %fusion.4 = f32[512,1536]{1,0:T(8,128)S(1)} fusion(bf16[512,3072]{1,0:T(8,128)(2,1)S(1)} %copy-done.24, bf16[3072,3072]{1,0:T(8,128)(2,1)} %param.4), kind=kOutput, calls=%fused_computation.4 | convolution fusion | flops 4831838208 | bytes 15728640 | tf_op jit(solution)/shard_map/dot_general | solution.py:143
  115.5 1.5 collective-permute-start.3
  117.0 0.7 collective-permute-start.1
  117.8 1.4 collective-permute-start.6
  119.3 0.6 collective-permute-start.4
  119.9 7.7 %collective-permute-done.3 = bf16[128,1536]{1,0:T(8,128)(2,1)S(1)} collective-permute-done((bf16[128,1536]{1,0:T(8,128)(2,1)S(1)}, bf16[128,1536]{1,0:T(8,128)(2,1)S(1)}, u32[]{:S(2)}, u32[]{:S(2)}) %collective-permute-start.3) | collective-permute-done | bytes 393248 | tf_op jit(solution)/shard_map/ppermute | solution.py:56
  128.1 0.7 collective-permute-start.11
  129.6 1.3 collective-permute-start.9
  130.9 1.0 pad_maximum_fusion.7
  131.8 20.3 %collective-permute-done.11 = bf16[128,1536]{1,0:T(8,128)(2,1)S(1)} collective-permute-done((bf16[128,1536]{1,0:T(8,128)(2,1)S(1)}, bf16[128,1536]{1,0:T(8,128)(2,1)S(1)}, u32[]{:S(2)}, u32[]{:S(2)}) %collective-permute-start.11) | collective-permute-done | bytes 393248 | tf_op jit(solution)/shard_map/ppermute | solution.py:56
  152.3 0.6 collective-permute-start.12
  153.1 0.9 collective-permute-start.10
  154.3 1.3 collective-permute-start.5
  155.8 0.9 fusion.47
  156.7 1.5 collective-permute-start.7
  158.2 20.5 %collective-permute-done.5 = bf16[128,1536]{1,0:T(8,128)(2,1)S(1)} collective-permute-done((bf16[128,1536]{1,0:T(8,128)(2,1)S(1)}, bf16[128,1536]{1,0:T(8,128)(2,1)S(1)}, u32[]{:S(2)}, u32[]{:S(2)}) %collective-permute-start.5) | collective-permute-done | bytes 393248 | tf_op jit(solution)/shard_map/ppermute | solution.py:56
  178.7 1.4 fusion.15
  180.1 1.5 collective-permute-start.8
  182.1 1.4 pad_maximum_fusion.3
  183.4 16.1 %fusion.55 = f32[512,3072]{1,0:T(8,128)} fusion(bf16[3072,3072]{1,0:T(8,128)(2,1)} %param.4, bf16[512,1536]{1,0:T(8,128)(2,1)S(1)} %bitcast.194, bf16[512,1536]{1,0:T(8,128)(2,1)} %bitcast.196), kind=kOutput, calls=%fused_computation.125 | convolution fusion | flops 9669967872 | bytes 28311552 | tf_op jit(solution)/shard_map/dot_general | solution.py:167
  199.5 2.2 fusion.8
  201.9 1.6 fusion.33
  203.5 1.0 collective-permute-start.15
  204.6 1.0 pad_maximum_fusion.8
  205.5 1.2 select_bitcast_fusion.15
  207.3 1.1 collective-permute-start.14
  208.5 7.0 %collective-permute-done.15 = bf16[128,1536]{1,0:T(8,128)(2,1)S(1)} collective-permute-done((bf16[128,1536]{1,0:T(8,128)(2,1)S(1)}, bf16[128,1536]{1,0:T(8,128)(2,1)S(1)}, u32[]{:S(2)}, u32[]{:S(2)}) %collective-permute-start.15) | collective-permute-done | bytes 393248 | tf_op jit(solution)/shard_map/ppermute | solution.py:56
  215.7 0.6 collective-permute-start.16
  216.3 1.1 fusion.48
  217.9 3.2 %collective-permute-start.20 = (bf16[64,3072]{1,0:T(8,128)(2,1)}, bf16[64,3072]{1,0:T(8,128)(2,1)}, u32[]{:S(2)}, u32[]{:S(2)}) collective-permute-start(bf16[64,3072]{1,0:T(8,128)(2,1)} %get-tuple-element.16), channel_id=1, source_target_pairs={{0,24},{4,28},{8,0},{12,4},{16,8},{20,12},{24,16},{28,20},{1,25},{... | collective-permute-start | bytes 1179656 | tf_op jit(solution)/shard_map/ppermute | solution.py:99
  221.2 10.8 %collective-permute-done.14 = bf16[2,128,1536]{2,1,0:T(8,128)(2,1)S(1)} collective-permute-done((bf16[2,128,1536]{2,1,0:T(8,128)(2,1)S(1)}, bf16[2,128,1536]{2,1,0:T(8,128)(2,1)S(1)}, u32[]{:S(2)}, u32[]{:S(2)}) %collective-permute-start.14) | collective-permute-done | bytes 786464 | tf_op jit(solution)/shard_map/ppermute | solution.py:56
  232.1 1.3 pad_maximum_fusion.5
  233.4 1.1 collective-permute-done.16
  234.5 1.3 pad_maximum_fusion.6
  235.8 16.4 %fusion.54 = f32[512,3072]{1,0:T(8,128)} fusion(bf16[3072,3072]{1,0:T(8,128)(2,1)} %param.4, bf16[512,1536]{1,0:T(8,128)(2,1)} %bitcast.200, bf16[512,1536]{1,0:T(8,128)(2,1)} %bitcast.198), kind=kOutput, calls=%fused_computation.124 | convolution fusion | flops 9669967872 | bytes 28311552 | tf_op jit(solution)/shard_map/dot_general | solution.py:167
  252.2 2.2 fusion.9
  254.5 1.3 pad_maximum_fusion.2
  255.9 2.1 fusion.43
  258.0 3.1 %pad_maximum_fusion = (bf16[512,3072]{1,0:T(8,128)(2,1)}, bf16[512,3072]{1,0:T(8,128)(2,1)}) fusion(bf16[512,1536]{1,0:T(8,128)(2,1)S(1)} %bitcast.195, bf16[512,1536]{1,0:T(8,128)(2,1)S(1)} %bitcast.197, bf16[512,1536]{1,0:T(8,128)(2,1)S(1)} %bitcast.201, bf16[512,1536]{1,0:T(8,128)(2,1)S(1)} %bitcast.199), kind=kLoop, calls=%fused_computation.8 | loop fusion | flops 12582912 | bytes 12582912 | tf_op jit(solution)/shard_map/concatenate | solution.py:166
  261.8 0.6 collective-permute-start.21
  262.4 3.3 %collective-permute-start.23 = (bf16[64,3072]{1,0:T(8,128)(2,1)S(1)}, bf16[64,3072]{1,0:T(8,128)(2,1)S(1)}, u32[]{:S(2)}, u32[]{:S(2)}) collective-permute-start(bf16[64,3072]{1,0:T(8,128)(2,1)S(1)} %get-tuple-element.19), channel_id=1, source_target_pairs={{0,24},{4,28},{8,0},{12,4},{16,8},{20,12},{24,16},{28,20},{1,25},{... | collective-permute-start | bytes 1179656 | tf_op jit(solution)/shard_map/ppermute | solution.py:99
  265.7 27.0 %shard_map.58 = f32[3072,3072]{1,0:T(8,128)} custom-call(bf16[512,3072]{1,0:T(8,128)(2,1)S(1)} %copy-done, bf16[512,3072]{1,0:T(8,128)(2,1)} %all-gather.5.cloned.1.call-done.refs_1_, bf16[512,3072]{1,0:T(8,128)(2,1)} %get-tuple-element.12.refs_2_, bf16[512,3072]{1,0:T(8,128)(2,1)} %get-tuple-element.13.refs_3_), custom_call_target="tpu_custom_call" | custom-call | flops 19327352832 | bytes 50331648 | tf_op jit(solution)/shard_map/pallas_call | solution.py:39
  292.7 6.6 %collective-permute-done.22 = bf16[64,3072]{1,0:T(8,128)(2,1)S(1)} collective-permute-done((bf16[64,3072]{1,0:T(8,128)(2,1)S(1)}, bf16[64,3072]{1,0:T(8,128)(2,1)S(1)}, u32[]{:S(2)}, u32[]{:S(2)}) %collective-permute-start.22) | collective-permute-done | bytes 393248 | tf_op jit(solution)/shard_map/ppermute | solution.py:99
  299.5 0.9 pad_maximum_fusion.13
  (100 shorter events, 5.8 us)
Async XLA Ops:
  7.2 44.1 %all-gather.3.cloned.1.call-start = ((), (), s32[]{:S(2)}) async-start(), calls=%async_computation | async-start | bytes 3538944 | tf_op jit(solution)/shard_map/all_gather | solution.py:133
  9.3 88.4 %all-gather.5.cloned.1.call-start = ((), (), s32[]{:S(2)}) async-start(), calls=%async_computation.1 | async-start | bytes 3538944 | tf_op jit(solution)/shard_map/all_gather | solution.py:133
  51.2 13.2 %copy-start = (bf16[512,3072]{1,0:T(8,128)(2,1)S(1)}, bf16[512,3072]{1,0:T(8,128)(2,1)}, u32[]{:S(2)}) copy-start(bf16[512,3072]{1,0:T(8,128)(2,1)} %all-gather.3.cloned.1.call-done.refs_0_) | copy-start | bytes 9437188
  61.0 1.9 copy-start.16
  62.9 13.2 %copy-start.20 = (bf16[256,3072]{1,0:T(8,128)(2,1)S(1)}, bf16[256,3072]{1,0:T(8,128)(2,1)}, u32[]{:S(2)}) copy-start(bf16[256,3072]{1,0:T(8,128)(2,1)} %param.5) | copy-start | bytes 4718596
  62.9 20.0 %collective-permute-start.2 = (bf16[2,128,1536]{2,1,0:T(8,128)(2,1)}, bf16[2,128,1536]{2,1,0:T(8,128)(2,1)}, u32[]{:S(2)}, u32[]{:S(2)}) collective-permute-start(bf16[2,128,1536]{2,1,0:T(8,128)(2,1)} %fusion.34), channel_id=1, source_target_pairs={{0,2},{1,3},{2,0},{3,1},{4,6},{5,7},{6,4},{7,5},{8,10},{9,11},{10,... | collective-permute-start | bytes 2359304 | tf_op jit(solution)/shard_map/ppermute | solution.py:56
  72.0 1.7 copy-start.14
  74.7 19.7 %collective-permute-start = (bf16[2,128,1536]{2,1,0:T(8,128)(2,1)}, bf16[2,128,1536]{2,1,0:T(8,128)(2,1)}, u32[]{:S(2)}, u32[]{:S(2)}) collective-permute-start(bf16[2,128,1536]{2,1,0:T(8,128)(2,1)} %fusion.36), channel_id=1, source_target_pairs={{0,1},{1,0},{2,3},{3,2},{4,5},{5,4},{6,7},{7,6},{8,9},{9,8},{10,11... | collective-permute-start | bytes 2359304 | tf_op jit(solution)/shard_map/ppermute | solution.py:56
  77.2 17.2 %copy-start.15 = (f32[512,1536]{1,0:T(8,128)S(1)}, f32[512,1536]{1,0:T(8,128)}, u32[]{:S(2)}) copy-start(f32[512,1536]{1,0:T(8,128)} %copy-done.14) | copy-start | bytes 9437188
  84.8 1.3 copy-start.9
  95.8 1.1 copy-start.7
  97.7 9.8 %copy-start.24 = (bf16[512,3072]{1,0:T(8,128)(2,1)S(1)}, bf16[512,3072]{1,0:T(8,128)(2,1)}, u32[]{:S(2)}) copy-start(bf16[512,3072]{1,0:T(8,128)(2,1)} %all-gather.5.cloned.1.call-done.refs_1_) | copy-start | bytes 9437188
  107.5 7.9 %copy-start.23 = (bf16[128,1536]{1,0:T(8,128)(2,1)S(1)}, bf16[128,1536]{1,0:T(8,128)(2,1)}, u32[]{:S(2)}) copy-start(bf16[128,1536]{1,0:T(8,128)(2,1)} %fusion.45) | copy-start | bytes 1179652
  107.5 9.5 %copy-start.22 = (bf16[128,1536]{1,0:T(8,128)(2,1)S(1)}, bf16[128,1536]{1,0:T(8,128)(2,1)}, u32[]{:S(2)}) copy-start(bf16[128,1536]{1,0:T(8,128)(2,1)} %fusion.44) | copy-start | bytes 1179652
  107.5 20.1 %copy-start.19 = (bf16[2,1,64,1536]{3,2,1,0:T(8,128)(2,1)S(1)}, bf16[2,1,64,1536]{3,2,1,0:T(8,128)(2,1)}, u32[]{:S(2)}) copy-start(bf16[2,1,64,1536]{3,2,1,0:T(8,128)(2,1)} %get-tuple-element.33) | copy-start | bytes 1179652
  115.4 12.2 %copy-start.10 = (f32[2,128,1536]{2,1,0:T(8,128)S(1)}, f32[2,128,1536]{2,1,0:T(8,128)}, u32[]{:S(2)}) copy-start(f32[2,128,1536]{2,1,0:T(8,128)} %copy-done.9) | copy-start | bytes 4718596
  115.5 13.6 %copy-start.8 = (f32[2,128,1536]{2,1,0:T(8,128)S(1)}, f32[2,128,1536]{2,1,0:T(8,128)}, u32[]{:S(2)}) copy-start(f32[2,128,1536]{2,1,0:T(8,128)} %copy-done.7) | copy-start | bytes 4718596
  115.5 13.6 %copy-start.18 = (bf16[2,1,64,1536]{3,2,1,0:T(8,128)(2,1)S(1)}, bf16[2,1,64,1536]{3,2,1,0:T(8,128)(2,1)}, u32[]{:S(2)}) copy-start(bf16[2,1,64,1536]{3,2,1,0:T(8,128)(2,1)} %get-tuple-element.34) | copy-start | bytes 1179652
  115.5 12.1 %collective-permute-start.3 = (bf16[128,1536]{1,0:T(8,128)(2,1)S(1)}, bf16[128,1536]{1,0:T(8,128)(2,1)S(1)}, u32[]{:S(2)}, u32[]{:S(2)}) collective-permute-start(bf16[128,1536]{1,0:T(8,128)(2,1)S(1)} %copy-done.23), channel_id=1, source_target_pairs={{0,1},{1,0},{2,3},{3,2},{4,5},{5,4},{6,7},{7,6},{8,9},{9,8},{10,11... | collective-permute-start | bytes 1179656 | tf_op jit(solution)/shard_map/ppermute | solution.py:56
  117.0 12.1 %collective-permute-start.1 = (bf16[128,1536]{1,0:T(8,128)(2,1)S(1)}, bf16[128,1536]{1,0:T(8,128)(2,1)S(1)}, u32[]{:S(2)}, u32[]{:S(2)}) collective-permute-start(bf16[128,1536]{1,0:T(8,128)(2,1)S(1)} %copy-done.22), channel_id=1, source_target_pairs={{0,2},{1,3},{2,0},{3,1},{4,6},{5,7},{6,4},{7,5},{8,10},{9,11},{10,... | collective-permute-start | bytes 1179656 | tf_op jit(solution)/shard_map/ppermute | solution.py:56
  117.8 37.8 %collective-permute-start.6 = (bf16[2,128,1536]{2,1,0:T(8,128)(2,1)S(1)}, bf16[2,128,1536]{2,1,0:T(8,128)(2,1)S(1)}, u32[]{:S(2)}, u32[]{:S(2)}) collective-permute-start(bf16[2,128,1536]{2,1,0:T(8,128)(2,1)S(1)} %fusion.35), channel_id=1, source_target_pairs={{0,2},{1,3},{2,0},{3,1},{4,6},{5,7},{6,4},{7,5},{8,10},{9,11},{10,... | collective-permute-start | bytes 2359304 | tf_op jit(solution)/shard_map/ppermute | solution.py:56
  119.3 34.7 %collective-permute-start.4 = (bf16[2,128,1536]{2,1,0:T(8,128)(2,1)S(1)}, bf16[2,128,1536]{2,1,0:T(8,128)(2,1)S(1)}, u32[]{:S(2)}, u32[]{:S(2)}) collective-permute-start(bf16[2,128,1536]{2,1,0:T(8,128)(2,1)S(1)} %fusion.37), channel_id=1, source_target_pairs={{0,1},{1,0},{2,3},{3,2},{4,5},{5,4},{6,7},{7,6},{8,9},{9,8},{10,11... | collective-permute-start | bytes 2359304 | tf_op jit(solution)/shard_map/ppermute | solution.py:56
  128.1 24.1 %collective-permute-start.11 = (bf16[128,1536]{1,0:T(8,128)(2,1)S(1)}, bf16[128,1536]{1,0:T(8,128)(2,1)S(1)}, u32[]{:S(2)}, u32[]{:S(2)}) collective-permute-start(bf16[128,1536]{1,0:T(8,128)(2,1)S(1)} %get-tuple-element.25), channel_id=1, source_target_pairs={{0,2},{1,3},{2,0},{3,1},{4,6},{5,7},{6,4},{7,5},{8,10},{9,11},{10,... | collective-permute-start | bytes 1179656 | tf_op jit(solution)/shard_map/ppermute | solution.py:56
  129.6 23.4 %collective-permute-start.9 = (bf16[128,1536]{1,0:T(8,128)(2,1)S(1)}, bf16[128,1536]{1,0:T(8,128)(2,1)S(1)}, u32[]{:S(2)}, u32[]{:S(2)}) collective-permute-start(bf16[128,1536]{1,0:T(8,128)(2,1)S(1)} %get-tuple-element.23), channel_id=1, source_target_pairs={{0,1},{1,0},{2,3},{3,2},{4,5},{5,4},{6,7},{7,6},{8,9},{9,8},{10,11... | collective-permute-start | bytes 1179656 | tf_op jit(solution)/shard_map/ppermute | solution.py:56
  152.3 29.2 %collective-permute-start.12 = (bf16[2,128,1536]{2,1,0:T(8,128)(2,1)S(1)}, bf16[2,128,1536]{2,1,0:T(8,128)(2,1)S(1)}, u32[]{:S(2)}, u32[]{:S(2)}) collective-permute-start(bf16[2,128,1536]{2,1,0:T(8,128)(2,1)S(1)} %pad_maximum_fusion.11), channel_id=1, source_target_pairs={{0,1},{1,0},{2,3},{3,2},{4,5},{5,4},{6,7},{7,6},{8,9},{9,8},{10,11... | collective-permute-start | bytes 2359304 | tf_op jit(solution)/shard_map/ppermute | solution.py:56
  153.1 28.8 %collective-permute-start.10 = (bf16[2,128,1536]{2,1,0:T(8,128)(2,1)S(1)}, bf16[2,128,1536]{2,1,0:T(8,128)(2,1)S(1)}, u32[]{:S(2)}, u32[]{:S(2)}) collective-permute-start(bf16[2,128,1536]{2,1,0:T(8,128)(2,1)S(1)} %pad_maximum_fusion.10), channel_id=1, source_target_pairs={{0,2},{1,3},{2,0},{3,1},{4,6},{5,7},{6,4},{7,5},{8,10},{9,11},{10,... | collective-permute-start | bytes 2359304 | tf_op jit(solution)/shard_map/ppermute | solution.py:56
  154.2 24.5 %copy-start.17 = (bf16[2,1,64,1536]{3,2,1,0:T(8,128)(2,1)S(1)}, bf16[2,1,64,1536]{3,2,1,0:T(8,128)(2,1)}, u32[]{:S(2)}) copy-start(bf16[2,1,64,1536]{3,2,1,0:T(8,128)(2,1)} %get-tuple-element.31) | copy-start | bytes 1179652
  154.3 24.4 %collective-permute-start.5 = (bf16[128,1536]{1,0:T(8,128)(2,1)S(1)}, bf16[128,1536]{1,0:T(8,128)(2,1)S(1)}, u32[]{:S(2)}, u32[]{:S(2)}) collective-permute-start(bf16[128,1536]{1,0:T(8,128)(2,1)S(1)} %fusion.46), channel_id=1, source_target_pairs={{0,2},{1,3},{2,0},{3,1},{4,6},{5,7},{6,4},{7,5},{8,10},{9,11},{10,... | collective-permute-start | bytes 1179656 | tf_op jit(solution)/shard_map/ppermute | solution.py:56
  155.8 25.9 %copy-start.5 = (f32[2,128,1536]{2,1,0:T(8,128)}, f32[2,128,1536]{2,1,0:T(8,128)S(1)}, u32[]{:S(2)}) copy-start(f32[2,128,1536]{2,1,0:T(8,128)S(1)} %bitcast_add_fusion.2) | copy-start | bytes 4718596
  156.7 45.2 %collective-permute-start.7 = (bf16[128,1536]{1,0:T(8,128)(2,1)}, bf16[128,1536]{1,0:T(8,128)(2,1)}, u32[]{:S(2)}, u32[]{:S(2)}) collective-permute-start(bf16[128,1536]{1,0:T(8,128)(2,1)} %fusion.47), channel_id=1, source_target_pairs={{0,1},{1,0},{2,3},{3,2},{4,5},{5,4},{6,7},{7,6},{8,9},{9,8},{10,11... | collective-permute-start | bytes 1179656 | tf_op jit(solution)/shard_map/ppermute | solution.py:56
  180.1 25.5 %collective-permute-start.8 = (bf16[128,1536]{1,0:T(8,128)(2,1)}, bf16[128,1536]{1,0:T(8,128)(2,1)}, u32[]{:S(2)}, u32[]{:S(2)}) collective-permute-start(bf16[128,1536]{1,0:T(8,128)(2,1)} %get-tuple-element.21), channel_id=1, source_target_pairs={{0,1},{1,0},{2,3},{3,2},{4,5},{5,4},{6,7},{7,6},{8,9},{9,8},{10,11... | collective-permute-start | bytes 1179656 | tf_op jit(solution)/shard_map/ppermute | solution.py:56
  199.5 2.4 copy-start.6
  199.5 5.0 %copy-start.21 = (bf16[128,1536]{1,0:T(8,128)(2,1)S(1)}, bf16[128,1536]{1,0:T(8,128)(2,1)}, u32[]{:S(2)}) copy-start(bf16[128,1536]{1,0:T(8,128)(2,1)} %get-tuple-element.22) | copy-start | bytes 1179652
  201.8 5.0 %collective-permute-start.13 = (bf16[4,64,3072]{2,1,0:T(8,128)(2,1)S(1)}, bf16[4,64,3072]{2,1,0:T(8,128)(2,1)S(1)}, u32[]{:S(2)}, u32[]{:S(2)}) collective-permute-start(bf16[4,64,3072]{2,1,0:T(8,128)(2,1)S(1)} %fusion.8), channel_id=1, source_target_pairs={{0,4},{4,0},{8,12},{12,8},{16,20},{20,16},{24,28},{28,24},{1,5},{5... | collective-permute-start | bytes 4718600 | tf_op jit(solution)/shard_map/ppermute | solution.py:88
  201.9 4.9 %copy-start.11 = (f32[512,3072]{1,0:T(8,128)S(1)}, f32[512,3072]{1,0:T(8,128)}, u32[]{:S(2)}) copy-start(f32[512,3072]{1,0:T(8,128)} %fusion.55) | copy-start | bytes 18874372
  203.5 12.0 %collective-permute-start.15 = (bf16[128,1536]{1,0:T(8,128)(2,1)S(1)}, bf16[128,1536]{1,0:T(8,128)(2,1)S(1)}, u32[]{:S(2)}, u32[]{:S(2)}) collective-permute-start(bf16[128,1536]{1,0:T(8,128)(2,1)S(1)} %get-tuple-element.27), channel_id=1, source_target_pairs={{0,2},{1,3},{2,0},{3,1},{4,6},{5,7},{6,4},{7,5},{8,10},{9,11},{10,... | collective-permute-start | bytes 1179656 | tf_op jit(solution)/shard_map/ppermute | solution.py:56
  207.3 24.7 %copy-start.1 = (f32[4,64,3072]{2,1,0:T(8,128)}, f32[4,64,3072]{2,1,0:T(8,128)S(1)}, u32[]{:S(2)}) copy-start(f32[4,64,3072]{2,1,0:T(8,128)S(1)} %bitcast_add_fusion.1) | copy-start | bytes 9437188
  207.3 24.6 %collective-permute-start.14 = (bf16[2,128,1536]{2,1,0:T(8,128)(2,1)S(1)}, bf16[2,128,1536]{2,1,0:T(8,128)(2,1)S(1)}, u32[]{:S(2)}, u32[]{:S(2)}) collective-permute-start(bf16[2,128,1536]{2,1,0:T(8,128)(2,1)S(1)} %pad_maximum_fusion.9), channel_id=1, source_target_pairs={{0,2},{1,3},{2,0},{3,1},{4,6},{5,7},{6,4},{7,5},{8,10},{9,11},{10,... | collective-permute-start | bytes 2359304 | tf_op jit(solution)/shard_map/ppermute | solution.py:56
  215.7 18.8 %collective-permute-start.16 = (bf16[2,128,1536]{2,1,0:T(8,128)(2,1)S(1)}, bf16[2,128,1536]{2,1,0:T(8,128)(2,1)S(1)}, u32[]{:S(2)}, u32[]{:S(2)}) collective-permute-start(bf16[2,128,1536]{2,1,0:T(8,128)(2,1)S(1)} %pad_maximum_fusion.12), channel_id=1, source_target_pairs={{0,1},{1,0},{2,3},{3,2},{4,5},{5,4},{6,7},{7,6},{8,9},{9,8},{10,11... | collective-permute-start | bytes 2359304 | tf_op jit(solution)/shard_map/ppermute | solution.py:56
  217.3 38.5 %collective-permute-start.18 = (bf16[64,3072]{1,0:T(8,128)(2,1)}, bf16[64,3072]{1,0:T(8,128)(2,1)S(1)}, u32[]{:S(2)}, u32[]{:S(2)}) collective-permute-start(bf16[64,3072]{1,0:T(8,128)(2,1)} %get-tuple-element.15), channel_id=1, source_target_pairs={{0,8},{4,12},{8,16},{12,20},{16,24},{20,28},{24,0},{28,4},{1,9},{5... | collective-permute-start | bytes 1179656 | tf_op jit(solution)/shard_map/ppermute | solution.py:99
  217.9 37.9 %collective-permute-start.20 = (bf16[64,3072]{1,0:T(8,128)(2,1)}, bf16[64,3072]{1,0:T(8,128)(2,1)}, u32[]{:S(2)}, u32[]{:S(2)}) collective-permute-start(bf16[64,3072]{1,0:T(8,128)(2,1)} %get-tuple-element.16), channel_id=1, source_target_pairs={{0,24},{4,28},{8,0},{12,4},{16,8},{20,12},{24,16},{28,20},{1,25},{... | collective-permute-start | bytes 1179656 | tf_op jit(solution)/shard_map/ppermute | solution.py:99
  221.2 34.7 %collective-permute-start.19 = (bf16[64,3072]{1,0:T(8,128)(2,1)}, bf16[64,3072]{1,0:T(8,128)(2,1)}, u32[]{:S(2)}, u32[]{:S(2)}) collective-permute-start(bf16[64,3072]{1,0:T(8,128)(2,1)} %get-tuple-element.17), channel_id=1, source_target_pairs={{0,16},{4,20},{8,24},{12,28},{16,0},{20,4},{24,8},{28,12},{1,17},{... | collective-permute-start | bytes 1179656 | tf_op jit(solution)/shard_map/ppermute | solution.py:99
  252.2 2.3 copy-start.12
  252.2 2.3 copy-start.13
  254.4 3.6 %copy-start.2 = (bf16[2,2,128,1536]{3,2,1,0:T(8,128)(2,1)S(1)}, bf16[2,2,128,1536]{3,2,1,0:T(8,128)(2,1)}, u32[]{:S(2)}) copy-start(bf16[2,2,128,1536]{3,2,1,0:T(8,128)(2,1)} %pad_maximum_fusion.3) | copy-start | bytes 4718596
  254.4 3.6 %copy-start.3 = (bf16[2,2,128,1536]{3,2,1,0:T(8,128)(2,1)S(1)}, bf16[2,2,128,1536]{3,2,1,0:T(8,128)(2,1)}, u32[]{:S(2)}) copy-start(bf16[2,2,128,1536]{3,2,1,0:T(8,128)(2,1)} %pad_maximum_fusion.5) | copy-start | bytes 4718596
  254.4 3.6 %copy-start.4 = (bf16[2,2,128,1536]{3,2,1,0:T(8,128)(2,1)S(1)}, bf16[2,2,128,1536]{3,2,1,0:T(8,128)(2,1)}, u32[]{:S(2)}) copy-start(bf16[2,2,128,1536]{3,2,1,0:T(8,128)(2,1)} %pad_maximum_fusion.6) | copy-start | bytes 4718596
  254.4 6.7 %collective-permute-start.17 = (bf16[4,64,3072]{2,1,0:T(8,128)(2,1)S(1)}, bf16[4,64,3072]{2,1,0:T(8,128)(2,1)S(1)}, u32[]{:S(2)}, u32[]{:S(2)}) collective-permute-start(bf16[4,64,3072]{2,1,0:T(8,128)(2,1)S(1)} %fusion.9), channel_id=1, source_target_pairs={{0,4},{4,0},{8,12},{12,8},{16,20},{20,16},{24,28},{28,24},{1,5},{5... | collective-permute-start | bytes 4718600 | tf_op jit(solution)/shard_map/ppermute | solution.py:88
  255.8 5.3 %slice-start = ((s8[6291456]{0:T(1024)(128)(4,1)}), s8[4194304]{0:T(1024)(128)(4,1)S(1)}, s32[]{:S(2)}) async-start(s8[6291456]{0:T(1024)(128)(4,1)} %bitcast.205), calls=%async_computation.2 | async-start | bytes 8388608
  258.0 3.1 %slice-start.1 = ((s8[6291456]{0:T(1024)(128)(4,1)}), s8[2097152]{0:T(1024)(128)(4,1)S(1)}, s32[]{:S(2)}) async-start(s8[6291456]{0:T(1024)(128)(4,1)} %bitcast.205), calls=%async_computation.3 | async-start | bytes 4194304
  261.8 30.9 %collective-permute-start.21 = (bf16[64,3072]{1,0:T(8,128)(2,1)S(1)}, bf16[64,3072]{1,0:T(8,128)(2,1)S(1)}, u32[]{:S(2)}, u32[]{:S(2)}) collective-permute-start(bf16[64,3072]{1,0:T(8,128)(2,1)S(1)} %get-tuple-element.18), channel_id=1, source_target_pairs={{0,8},{4,12},{8,16},{12,20},{16,24},{20,28},{24,0},{28,4},{1,9},{5... | collective-permute-start | bytes 1179656 | tf_op jit(solution)/shard_map/ppermute | solution.py:99
  262.4 30.3 %collective-permute-start.23 = (bf16[64,3072]{1,0:T(8,128)(2,1)S(1)}, bf16[64,3072]{1,0:T(8,128)(2,1)S(1)}, u32[]{:S(2)}, u32[]{:S(2)}) collective-permute-start(bf16[64,3072]{1,0:T(8,128)(2,1)S(1)} %get-tuple-element.19), channel_id=1, source_target_pairs={{0,24},{4,28},{8,0},{12,4},{16,8},{20,12},{24,16},{28,20},{1,25},{... | collective-permute-start | bytes 1179656 | tf_op jit(solution)/shard_map/ppermute | solution.py:99
  265.7 33.6 %collective-permute-start.22 = (bf16[64,3072]{1,0:T(8,128)(2,1)S(1)}, bf16[64,3072]{1,0:T(8,128)(2,1)S(1)}, u32[]{:S(2)}, u32[]{:S(2)}) collective-permute-start(bf16[64,3072]{1,0:T(8,128)(2,1)S(1)} %get-tuple-element.20), channel_id=1, source_target_pairs={{0,16},{4,20},{8,24},{12,28},{16,0},{20,4},{24,8},{28,12},{1,17},{... | collective-permute-start | bytes 1179656 | tf_op jit(solution)/shard_map/ppermute | solution.py:99
Sparse Core Ops, SparseCore 0:
  10.2 40.9 all-gather.2
  52.9 37.1 all-gather.4
